TPU v7x, 32 devices: a whole 2x2x4 slice. The times are simulated.
32 devices in a mesh: grp: 2 (over x), dev: 16 (over z, y, core).
Axes of the slice: x: 2, y: 2, z: 4, core: 2. Of those that a mesh axis runs over, the one named last changes fastest.
Arguments:
- embeddings: bfloat16 [16384, 768], P(('grp', 'dev')), parts along dimension 0, as said below
- position: int32 [16384], P(('grp', 'dev')), parts along dimension 0, may hold values from 0 to 8191, as said below
- cluster_ids: int32 [16384], P(('grp', 'dev')), parts along dimension 0, may hold values from 0 to 8191, as said below
Outputs:
- weight: float32 [16384], P(('grp', 'dev')), parts along dimension 0
There are 2 independent parts, one for each index of `grp`. A program takes and returns all parts, laid end to end along the dimension named above; each array names one. Nothing has to cross between parts.
Inputs may be any that keep to these rules, and one draw needn't show every extreme that they name: `position`: a permutation; the 512 documents of every device take exactly 32 positions in the range of positions of every device. `cluster_ids`: never falling along positions; each cluster holds 1 to 2048 consecutive positions, and one holds exactly 2048; the cluster at the first position is numbered 0, the cluster at the last position 8191, and each other cluster one more than the cluster before it. `embeddings`: rows are not normalized.
All inputs are finite; a program needn't handle non-finite values.
Results may differ from a plain program's by a relative error of at most 0.0003.
Values may be sent and summed in bfloat16 or wider, within the bound.
No kernel may reach another device: no remote copies, remote signals or barrier semaphores. Data moves between devices by JAX's collectives and lax.ppermute only.
A program may use at most 64 MiB of HBM per device.

v0:
```python
import functools
import math

import jax
import jax.numpy as jnp
from jax import lax
from jax.experimental import pallas as pl
from jax.experimental.pallas import tpu as pltpu
from jax.sharding import PartitionSpec as P

MOST = 2048
HALF = MOST // 2
SIMILARITY_CUTOFF = 0.9
SOFTMAX_HEAT = 0.02
SCALE = math.log2(math.e) / SOFTMAX_HEAT
SHIFT = SIMILARITY_CUTOFF * SCALE
QUAD = 4
CHUNK = 256
LANES = 128
VMEM_LIMIT = 16 * 1024 * 1024

NT = (((1,), (1,)), ((), ()))
TN = (((0,), (0,)), ((), ()))


def iota(shape, dim):
    return lax.broadcasted_iota(jnp.int32, shape, dim)


def call(kernel, out_shape, limit=VMEM_LIMIT, **extra):
    return pl.pallas_call(
        kernel,
        out_shape=out_shape,
        compiler_params=pltpu.CompilerParams(vmem_limit_bytes=limit),
        **extra,
    )


def arrange_kernel(per_half, halves, position_hbm, rows_hbm, *refs):
    *outs, rank_ref, place, rows, sems = refs
    copies = [
        pltpu.make_async_copy(position_hbm, place, sems.at[0]),
        pltpu.make_async_copy(rows_hbm, rows, sems.at[1]),
    ]
    for copy in copies:
        copy.start()
    n = rows.shape[0]
    earlier = (iota((n, n), 0) < iota((n, n), 1)).astype(jnp.bfloat16)
    copies[0].wait()
    half = place[...] // HALF
    kinds = iota((halves, n), 0) == half
    counts = jnp.dot(kinds.astype(jnp.bfloat16), earlier, preferred_element_type=jnp.float32)
    count = jnp.sum(jnp.where(kinds, counts, 0.0), axis=0, keepdims=True).astype(jnp.int32)
    rank_ref[...] = half * per_half + count
    rank = half * per_half + count
    if len(outs) > 1:
        plane = (half // 2) ^ (lax.axis_index("dev") // QUAD)
        rank = (2 * plane + 1 - half % 2) * per_half + count
    pick = (iota((n, n), 0) == rank).astype(jnp.bfloat16)
    copies[1].wait()
    picked = jnp.dot(pick, rows[...], preferred_element_type=jnp.float32)
    at = 0
    for out in outs:
        out[...] = picked[at : at + out.shape[0], :].astype(out.dtype)
        at += out.shape[0]


def facts_kernel(per_half, position_ref, ids_ref, rank_ref, *refs):
    *pieces, out_ref = refs
    n = position_ref.shape[1]
    pick = iota((n, n), 0) == rank_ref[...]
    where_to = position_ref[...].astype(jnp.float32)
    column = jnp.sum(jnp.where(pick, where_to, 0.0), axis=1, keepdims=True)
    eye = iota((n, n), 0) == iota((n, n), 1)
    positions = jnp.sum(jnp.where(eye, column, 0.0), axis=0, keepdims=True)
    total = jnp.zeros((1, n), jnp.float32)
    k = 0
    for piece in pieces:
        size = n if len(pieces) == 1 else per_half
        for start in range(0, piece.shape[0], size):
            wide = piece[start : start + size, :].astype(jnp.float32)
            inverse = lax.rsqrt(jnp.sum(wide * wide, axis=1, keepdims=True) + 1e-06)
            first = 0
            if len(pieces) > 1:
                plane = (k // 2) ^ (lax.axis_index("dev") // QUAD)
                first = (2 * plane + 1 - k % 2) * per_half
            here = iota((size, n), 0) + first == iota((size, n), 1)
            total += jnp.sum(jnp.where(here, inverse, 0.0), axis=0, keepdims=True)
            k += 1
    ids = ids_ref[...].astype(jnp.float32)
    if len(out_ref.shape) == 2:
        for k, values in enumerate((positions, total, ids, jnp.zeros_like(ids))):
            out_ref[k : k + 1, :] = values
        return
    beyond = jnp.zeros((1, per_half), jnp.float32)
    ids = [ids[:, at : at + LANES] for at in range(0, n, LANES)]
    wide = [jnp.concatenate([beyond, values, beyond], axis=1) for values in (positions, total)]
    for peer in range(out_ref.shape[0]):
        at = peer // QUAD * LANES
        lines = [values[:, at + k : at + k + LANES] for values in wide for k in (0, LANES)]
        for k, line in enumerate(lines + ids):
            out_ref[peer, k : k + 1, :] = line


def labels_kernel(place_ref, table_ref, out_ref):
    place = place_ref[...]
    depth = table_ref.shape[0]
    n = place.shape[1]
    table = table_ref[...]
    high = jnp.floor(table * (1.0 / 256.0))
    low = table - high * 256.0
    line = (iota((depth, n), 0) == place // LANES).astype(jnp.bfloat16)
    high = lax.dot_general(
        high.astype(jnp.bfloat16), line, TN, preferred_element_type=jnp.float32
    )
    low = lax.dot_general(
        low.astype(jnp.bfloat16), line, TN, preferred_element_type=jnp.float32
    )
    here = iota((LANES, n), 0) == place % LANES
    out_ref[...] = jnp.sum(jnp.where(here, high * 256.0 + low, 0.0), axis=0, keepdims=True)


NAMES = ("b0h", "b0l", "b1h", "b1l", "b2h", "b2l", "u", "l", "u1", "l1")
SUMS = ("b0h", "b0l", "b2h", "b2l", "u", "l", "u1", "l1")


class Terms:
    def __init__(self, arrays, rows_ref, columns_ref, out_ref, last_ref):
        self.arrays, self.rows, self.columns, self.out = arrays, rows_ref, columns_ref, out_ref
        self.last = last_ref
        self.sums = {}

    def add(self, name, values):
        self.sums[name] = self.sums[name] + values if name in self.sums else values

    def job(self, down, across):
        n = self.arrays[down].shape[0]
        products = lax.dot_general(
            self.arrays[down][...],
            self.arrays[across][...],
            NT,
            preferred_element_type=jnp.float32,
        )
        at, to = NAMES.index(down) * n, NAMES.index(across) * n
        scale = self.columns[at : at + n, 0:1]
        label = self.columns[at : at + n, 1:2]
        power = products * scale * self.rows[0:1, to : to + n] - SHIFT
        mask = label == self.rows[1:2, to : to + n]
        if down == across:
            mask &= iota((n, n), 0) != iota((n, n), 1)
        values = jnp.where(mask, jnp.exp2(power), 0.0)
        self.add(across, jnp.sum(values, axis=0, keepdims=True))
        if down in ("u", "l", "u1", "l1") or (down, across) == ("b0h", "b0l"):
            side = jnp.zeros((n, LANES), jnp.float32)
            for lane in range(0, n, LANES):
                side += values[:, lane : lane + LANES]
            self.add(down, jnp.sum(side.T, axis=0, keepdims=True))

    def totals(self):
        totals = {}
        for k, name in enumerate(SUMS):
            values = self.sums.get(name)
            last = self.last[k : k + 1, :] if self.last is not None else None
            if values is None:
                n = self.arrays["b0l"].shape[0]
                values = jnp.zeros((1, n), jnp.float32) if last is None else last
            elif last is not None:
                values += last
            totals[name] = values
        return totals

    def write(self):
        for k, values in enumerate(self.totals().values()):
            self.out[k : k + 1, :] = values


def lay_out(sums, m, out_ref):
    me = lax.axis_index("dev")
    slab, lane = me // QUAD, me % QUAD
    even = slab % 2 == 0
    rows = iota((out_ref.shape[0], 2 * m), 0)
    own = jnp.zeros(rows.shape, jnp.float32)
    halo = own

    def piece(name, x):
        return sums[name][:, x * m : (x + 1) * m]

    for x in range(QUAD):
        row = (slab ^ x) * QUAD
        for line, lower, upper in ((0, "b0l", "b0h"), (2, "b2l", "b2h")):
            both = jnp.concatenate([piece(lower, x), piece(upper, x)], axis=1)
            own = jnp.where(rows == row + (lane ^ line), both, own)
        for line, before, after in ((0, "u", "l"), (1, "u1", "l1")):
            before = jnp.where(even, piece(before, x ^ 3), piece(before, x ^ 1))
            after = jnp.where(even, piece(after, x ^ 1), piece(after, x ^ 3))
            both = jnp.concatenate([before, after], axis=1)
            halo = jnp.where(rows == row + (lane ^ line), both, halo)
    out_ref[:, 0, :] = own
    out_ref[:, 1, :] = halo


def masses_call(jobs, arrays, rows, columns, last=None, layout=None):
    names = [name for name in NAMES if any(name in job for job in jobs)]

    def kernel(*refs):
        refs = list(refs)
        held = {name: refs.pop(0) for name in names}
        rows_ref, columns_ref = refs.pop(0), refs.pop(0)
        last_ref = refs.pop(0) if last is not None else None
        t = Terms(held, rows_ref, columns_ref, refs.pop(0), last_ref)
        for job in jobs:
            t.job(*job)
        if layout is None:
            t.write()
        else:
            lay_out(t.totals(), layout[2] // 2, t.out)

    operands = [arrays[name] for name in names] + [rows, columns]
    if last is not None:
        operands.append(last)
    n, width = operands[0].shape
    return call(
        kernel,
        jax.ShapeDtypeStruct(layout or (len(SUMS), n), jnp.float32),
        cost_estimate=pl.CostEstimate(flops=0, transcendentals=0, bytes_accessed=0),
    )(*operands)


def weights_kernel(rank_ref, returned_ref, out_ref):
    peers, _, width = returned_ref.shape
    m = width // 2
    rank = rank_ref[...]
    n = rank.shape[1]
    slab, upper, member = rank // width, rank // m % 2 == 1, rank % m
    plane = iota((peers, n), 0) // QUAD

    def chosen(k, which, column):
        picked = lax.dot_general(
            returned_ref[:, k, :],
            jnp.where(plane == which, 1.0, 0.0),
            TN,
            precision=lax.Precision.HIGHEST,
            preferred_element_type=jnp.float32,
        )
        here = iota((width, n), 0) == column
        return jnp.sum(jnp.where(here, picked, 0.0), axis=0, keepdims=True)

    mass = chosen(0, slab, jnp.where(upper, m + member, member))
    mass += chosen(1, jnp.where(upper, slab + 1, slab - 1), jnp.where(upper, member, m + member))
    out_ref[...] = 1.0 / (1.0 + mass)


def xor_order(array, axis, bits):
    count = array.shape[axis]
    for k in range(count.bit_length() - 1):
        step = 1 << k
        shape = array.shape[:axis] + (count // (2 * step), 2, step) + array.shape[axis + 1 :]
        split = array.reshape(shape)
        split = jnp.where((bits >> k) & 1 == 1, jnp.flip(split, axis + 1), split)
        array = split.reshape(array.shape)
    return array


def shards(embeddings, position, cluster_ids):
    n, width = embeddings.shape
    peers = lax.axis_size("dev")
    me = lax.axis_index("dev")
    planes = peers // QUAD
    slab, lane = me // QUAD, me % QUAD
    per_half = n // (2 * planes)
    by_permutes = planes == 4
    pieces = [per_half] * 2 + [2 * per_half] + [per_half] * 4 if by_permutes else [n]
    f32 = jnp.float32

    def swapped(rows_, bit):
        return lax.ppermute(rows_, "dev", [(i, i ^ bit) for i in range(peers)])

    def passed(rows_, by):
        pairs = [(i, i + by) for i in range(peers) if 0 <= i + by < peers]
        return lax.ppermute(rows_, "dev", pairs)

    def after_all(value, *others):
        return lax.optimization_barrier((value, *others))[0]

    def as_received(values, axis, plane):
        return xor_order(values, axis, plane) if by_permutes else values

    where_to = position.reshape(1, n)
    in_hbm = pl.BlockSpec(memory_space=pltpu.HBM)
    *arranged, rank = call(
        functools.partial(arrange_kernel, per_half, 2 * planes),
        [jax.ShapeDtypeStruct((size, width), embeddings.dtype) for size in pieces]
        + [jax.ShapeDtypeStruct((1, n), jnp.int32)],
        in_specs=[in_hbm, in_hbm],
        scratch_shapes=[
            pltpu.VMEM((1, n), jnp.int32),
            pltpu.VMEM((n, width), embeddings.dtype),
            pltpu.SemaphoreType.DMA((2,)),
        ],
    )(where_to, embeddings)
    if by_permutes:
        own_upper, own_lower, to_1, upper_2, lower_2, upper_3, lower_3 = arranged
        upper_3 = swapped(upper_3, 3 * QUAD)
        upper_2 = swapped(upper_2, 2 * QUAD)
        both_1 = swapped(to_1, QUAD)
        lower_3 = swapped(lower_3, 3 * QUAD)
        lower_2 = swapped(lower_2, 2 * QUAD)
        upper = jnp.concatenate([own_upper, both_1[:per_half], upper_2, upper_3], axis=0)
        lower = jnp.concatenate([own_lower, both_1[per_half:], lower_2, lower_3], axis=0)
    else:
        lines = [[p * QUAD + q for p in range(planes)] for q in range(QUAD)]
        block = lax.all_to_all(
            arranged[0], "dev", split_axis=0, concat_axis=0, axis_index_groups=lines, tiled=True
        ).reshape(planes, 2, per_half, width)
        upper = block[:, 1].reshape(n // 2, width)
        lower = block[:, 0].reshape(n // 2, width)

    aligned = by_permutes and 2 * per_half == LANES
    own_facts = (where_to, cluster_ids.reshape(1, n), rank, *arranged)
    facts_shape = (peers, 4 + n // LANES, LANES) if aligned else (4, n)
    facts = call(
        functools.partial(facts_kernel, per_half), jax.ShapeDtypeStruct(facts_shape, f32)
    )(*own_facts)
    if not aligned:
        seen = jnp.pad(facts[:2], ((0, 0), (per_half, per_half)))
        seen = jnp.stack(
            [seen[:, 2 * p * per_half : (2 * p + 4) * per_half] for p in range(planes)]
        ).reshape(planes, 1, 8 * per_half)
        facts = jnp.concatenate(
            [
                jnp.broadcast_to(seen, (planes, QUAD, 8 * per_half)),
                jnp.broadcast_to(facts[2], (planes, QUAD, n)),
            ],
            axis=2,
        )
        facts = facts.reshape(peers, 8 * per_half + n)
    facts = after_all(facts, both_1 if by_permutes else block)
    facts = lax.all_to_all(facts, "dev", split_axis=0, concat_axis=0, tiled=True)
    arrays = {"b0h": upper}
    arrays["b2h"] = swapped(upper, 2)
    arrays["b1h"] = swapped(upper, 1)
    lower = after_all(lower, arrays["b1h"])
    arrays["b0l"] = lower
    arrays["u"] = passed(upper, QUAD)
    arrays["b2l"] = swapped(lower, 2)
    arrays["l"] = passed(lower, -QUAD)
    arrays["b1l"] = swapped(lower, 1)

    if aligned:
        ids, near = facts[:, 4:].reshape(peers * n), facts[:, :4]
    else:
        ids, near = facts[:, 8 * per_half :].reshape(peers * n), facts[:, : 8 * per_half]
    ids = jnp.pad(ids, (MOST, MOST))
    ids = lax.dynamic_slice_in_dim(ids, slab * MOST, 3 * MOST, 0)
    near = near.reshape(planes, QUAD, 2, 4, per_half)
    near = xor_order(near, 1, lane).transpose(2, 1, 3, 0, 4)
    before = as_received(near[:, :2, 0], 2, slab - 1)
    after = as_received(near[:, :2, 3], 2, slab + 1)
    own = as_received(near[:, :3, 1:3], 3, slab)
    near = jnp.concatenate(
        [
            jnp.stack([own[:, :, 1], own[:, :, 0]], axis=2).reshape(2, 3 * n),
            jnp.stack([before, after], axis=2).reshape(2, 2 * n),
        ],
        axis=1,
    )
    total = 5 * n
    place = near[0].astype(jnp.int32) - (slab - 1) * MOST
    label = call(labels_kernel, jax.ShapeDtypeStruct((1, total), f32))(
        place.reshape(1, total), ids.reshape(3 * MOST // LANES, LANES)
    )[0]
    at = jnp.arange(total)
    absent = (at >= 3 * n) & jnp.where(at % n >= n // 2, slab == planes - 1, slab == 0)
    label = jnp.where(absent, -1.0, label)
    rows = jnp.stack([near[1], label])
    columns = jnp.stack([near[1] * SCALE, label], axis=1)

    def masses_after(jobs, last=None):
        return masses_call(jobs, arrays, rows, columns, last)

    masses = masses_after(
        [("b0h", "b0h"), ("b1h", "b0h"), ("b2h", "b0h"), ("b1h", "b2h")]
        + [("b0l", "b0l"), ("b0h", "b0l"), ("b1h", "b0l"), ("b2h", "b0l")]
        + [("b1l", "b0h"), ("b1l", "b0l"), ("b1l", "b2h")]
    )
    arrays["u1"] = swapped(after_all(arrays['u'], arrays["b2h"]), 1)
    masses = masses_after([(u, b) for u in ("u", "u1") for b in ("b0h", "b0l", "b2h")], masses)
    arrays["l1"] = swapped(after_all(arrays["l"], masses, arrays["b2l"]), 1)
    masses = masses_after(
        [("b2l", "b0h"), ("b2l", "b0l"), ("b1h", "b2l"), ("b1l", "b2l"), ("u", "b2l"), ("u1", "b2l")],
        masses,
    )
    last = [("l", "b0l"), ("l", "b2l"), ("l1", "b0l"), ("l1", "b2l")]
    if by_permutes:
        outgoing = masses_call(last, arrays, rows, columns, masses, (peers, 2, 2 * per_half))
    else:
        masses = masses_after(last, masses)
        masses = masses.reshape(4, 2, planes, per_half)
        slabs = as_received(masses[:2], 2, slab)
        before = as_received(masses[2:, 0], 1, slab - 1)
        after = as_received(masses[2:, 1], 1, slab + 1)
        none = jnp.zeros_like(before[0])
        outgoing = jnp.stack(
            [
                jnp.stack([slabs[0, 1], none, slabs[1, 1], none]),
                jnp.stack([slabs[0, 0], none, slabs[1, 0], none]),
                jnp.stack([before[0], before[1], none, none]),
                jnp.stack([after[0], after[1], none, none]),
            ],
            axis=2,
        )
        outgoing = xor_order(outgoing, 0, lane).transpose(1, 0, 2, 3)
        outgoing = outgoing.reshape(peers, 2, 2 * per_half)
    returned = lax.all_to_all(outgoing, "dev", split_axis=0, concat_axis=0, tiled=True)
    weight = call(
        weights_kernel, jax.ShapeDtypeStruct((1, n), f32)
    )(rank, returned)
    return weight.reshape(n)


def solution(mesh):
    return jax.shard_map(
        shards,
        mesh=mesh,
        in_specs=(P(("grp", "dev"), None), P(("grp", "dev")), P(("grp", "dev"))),
        out_specs=P(("grp", "dev")),
        check_vma=False,
    )
```

profile of v0, /device:TPU:0, one launch (start us, length us, event | category | flops | bytes accessed | tf_op | source)
XLA Modules:
  0.0 59.5 jit_solution(8586202540459072095)
XLA Ops:
  0.0 0.0 copy-start
  0.0 1.1 %copy-done = bf16[512,768]{1,0:T(8,128)(2,1)S(1)} copy-done((bf16[512,768]{1,0:T(8,128)(2,1)S(1)}, bf16[512,768]{1,0:T(8,128)(2,1)}, u32[]{:S(2)}) %copy-start) | copy-done | bytes 786456
  1.1 0.0 copy-start.1
  1.1 0.7 %copy-done.1 = s32[512]{0:T(512)S(1)} copy-done((s32[512]{0:T(512)S(1)}, s32[512]{0:T(512)}, u32[]{:S(2)}) %copy-start.1) | copy-done | bytes 2072
  1.8 1.0 %shard_map.37 = (bf16[64,768]{1,0:T(8,128)(2,1)S(1)}, bf16[64,768]{1,0:T(8,128)(2,1)S(1)}, bf16[128,768]{1,0:T(8,128)(2,1)S(1)}, bf16[64,768]{1,0:T(8,128)(2,1)S...) custom-call(s32[1,512]{1,0:T(1,128)S(1)} %bitcast.27, ...), custom_call_target="tpu_custom_call" | custom-call | tf_op jit(solution)/shard_map/pallas_call | solution.py:290
  2.9 3.1 %collective-permute-start = (bf16[128,768]{1,0:T(8,128)(2,1)S(1)}, bf16[128,768]{1,0:T(8,128)(2,1)S(1)}, u32[]{:S(2)}, u32[]{:S(2)}) collective-permute-start(bf16[128,768]{1,0:T(8,128)(2,1)S(1)} %get-tuple-element.19.refs_2_), channel_id=1, source_target_pairs={{0,4},{1,5},{2,6},{3,7},{4,0},{5,1},{6,2},{7,3},{8,12},{9,13},{10,... | collective-permute-start | bytes 589832 | tf_op jit(solution)/shard_map/ppermute | solution.py:276
  5.9 2.6 %collective-permute-start.3 = (bf16[64,768]{1,0:T(8,128)(2,1)S(1)}, bf16[64,768]{1,0:T(8,128)(2,1)S(1)}, u32[]{:S(2)}, u32[]{:S(2)}) collective-permute-start(bf16[64,768]{1,0:T(8,128)(2,1)S(1)} %get-tuple-element.23.refs_3_), channel_id=1, source_target_pairs={{0,8},{1,9},{2,10},{3,11},{4,12},{5,13},{6,14},{7,15},{8,0},{9,1},... | collective-permute-start | bytes 294920 | tf_op jit(solution)/shard_map/ppermute | solution.py:276
  8.5 0.0 collective-permute-start.4
  8.5 1.9 %collective-permute-start.1 = (bf16[64,768]{1,0:T(8,128)(2,1)S(1)}, bf16[64,768]{1,0:T(8,128)(2,1)S(1)}, u32[]{:S(2)}, u32[]{:S(2)}) collective-permute-start(bf16[64,768]{1,0:T(8,128)(2,1)S(1)} %get-tuple-element.20.refs_4_), channel_id=1, source_target_pairs={{0,8},{1,9},{2,10},{3,11},{4,12},{5,13},{6,14},{7,15},{8,0},{9,1},... | collective-permute-start | bytes 294920 | tf_op jit(solution)/shard_map/ppermute | solution.py:276
  10.4 1.9 %collective-permute-start.2 = (bf16[64,768]{1,0:T(8,128)(2,1)S(1)}, bf16[64,768]{1,0:T(8,128)(2,1)S(1)}, u32[]{:S(2)}, u32[]{:S(2)}) collective-permute-start(bf16[64,768]{1,0:T(8,128)(2,1)S(1)} %get-tuple-element.21.refs_6_), channel_id=1, source_target_pairs={{0,12},{1,13},{2,14},{3,15},{4,8},{5,9},{6,10},{7,11},{8,4},{9,5},... | collective-permute-start | bytes 294920 | tf_op jit(solution)/shard_map/ppermute | solution.py:276
  12.4 0.0 copy-start.2
  12.4 0.7 %copy-done.2 = s32[512]{0:T(512)S(1)} copy-done((s32[512]{0:T(512)S(1)}, s32[512]{0:T(512)}, u32[]{:S(2)}) %copy-start.2) | copy-done | bytes 2072
  13.0 0.0 copy-start.3
  13.0 0.7 %copy-done.3 = s32[512]{0:T(512)S(1)} copy-done((s32[512]{0:T(512)S(1)}, s32[512]{0:T(512)}, u32[]{:S(2)}) %copy-start.3) | copy-done | bytes 2072
  13.7 1.2 %shard_map.38 = f32[16,8,128]{2,1,0:T(8,128)} custom-call(s32[1,512]{1,0:T(1,128)S(1)} %bitcast.28, s32[1,512]{1,0:T(1,128)S(1)} %bitcast.29, s32[1,512]{1,0:T(1,128)S(1)} %get-tuple-element.17.rank_ref, bf16[64,768]{1,0:T(8,128)(2,1)S(1)} %get-tuple-element.22.refs_0_, bf16[64,768]{1,0:T(8,128)(2,1)S(1)} %get-tuple-element.18.refs_1_, ...), custom_call_target="tpu_custom_call" | custom-call | tf_op jit(solution)/shard_map/pallas_call | solution.py:321
  14.9 0.0 collective-permute-done
  14.9 5.0 %all-to-all-start = ((f32[16,8,128]{2,1,0:T(8,128)}), f32[16,8,128]{2,1,0:T(8,128)S(1)}, u32[]{:S(2)}, u32[]{:S(2)}) async-start(f32[16,8,128]{2,1,0:T(8,128)} %shard_map.38), calls=%async_computation | async-start | bytes 131072 | tf_op jit(solution)/shard_map/all_to_all | solution.py:338
  20.0 0.0 collective-permute-done.3
  20.0 0.0 collective-permute-done.4
  20.0 0.5 collective-permute-start.5
  20.5 1.7 %collective-permute-start.8 = (bf16[256,768]{1,0:T(8,128)(2,1)S(1)}, bf16[256,768]{1,0:T(8,128)(2,1)S(1)}, u32[]{:S(2)}, u32[]{:S(2)}) collective-permute-start(bf16[256,768]{1,0:T(8,128)(2,1)S(1)} %pad_maximum_fusion.1.refs_0_), channel_id=1, source_target_pairs={{0,2},{1,3},{2,0},{3,1},{4,6},{5,7},{6,4},{7,5},{8,10},{9,11},{10,... | collective-permute-start | bytes 1179656 | tf_op jit(solution)/shard_map/ppermute | solution.py:276
  22.2 5.1 %collective-permute-start.9 = (bf16[256,768]{1,0:T(8,128)(2,1)S(1)}, bf16[256,768]{1,0:T(8,128)(2,1)S(1)}, u32[]{:S(2)}, u32[]{:S(2)}) collective-permute-start(bf16[256,768]{1,0:T(8,128)(2,1)S(1)} %pad_maximum_fusion.1.refs_0_), channel_id=1, source_target_pairs={{0,4},{1,5},{2,6},{3,7},{4,8},{5,9},{6,10},{7,11},{8,12},{9,13},{1... | collective-permute-start | bytes 1179656 | tf_op jit(solution)/shard_map/ppermute | solution.py:280
  27.2 0.0 collective-permute-done.1
  27.2 0.0 collective-permute-done.2
  27.3 1.0 %all-to-all-done = f32[16,8,128]{2,1,0:T(8,128)S(1)} async-done(((f32[16,8,128]{2,1,0:T(8,128)}), f32[16,8,128]{2,1,0:T(8,128)S(1)}, u32[]{:S(2)}, u32[]{:S(2)}) %all-to-all-start) | async-done | bytes 65568 | tf_op jit(solution)/shard_map/all_to_all | solution.py:338
  28.3 0.1 reshape_reshape.15
  28.6 0.1 reshape.133
  28.7 0.1 rev.32
  28.9 0.1 reshape.132
  29.0 0.6 %shard_map.39 = f32[1,2560]{1,0:T(1,128)S(1)} custom-call(s32[1,2560]{1,0:T(1,128)S(1)} %fusion.2.place_ref, f32[48,128]{1,0:T(8,128)S(1)} %fusion.1.table_ref), custom_call_target="tpu_custom_call" | custom-call | tf_op jit(solution)/shard_map/pallas_call | solution.py:369
  29.7 0.0 collective-permute-done.5.refs_2_
  29.7 0.1 collective-permute-start.11
  29.8 0.6 %collective-permute-start.6 = (bf16[256,768]{1,0:T(8,128)(2,1)S(1)}, bf16[256,768]{1,0:T(8,128)(2,1)}, u32[]{:S(2)}, u32[]{:S(2)}) collective-permute-start(bf16[256,768]{1,0:T(8,128)(2,1)S(1)} %pad_maximum_fusion.refs_1_.refs_0_), channel_id=1, source_target_pairs={{0,2},{1,3},{2,0},{3,1},{4,6},{5,7},{6,4},{7,5},{8,10},{9,11},{10,... | collective-permute-start | bytes 1179656 | tf_op jit(solution)/shard_map/ppermute | solution.py:276
  30.4 1.3 %collective-permute-start.7 = (bf16[256,768]{1,0:T(8,128)(2,1)S(1)}, bf16[256,768]{1,0:T(8,128)(2,1)}, u32[]{:S(2)}, u32[]{:S(2)}) collective-permute-start(bf16[256,768]{1,0:T(8,128)(2,1)S(1)} %pad_maximum_fusion.refs_1_.refs_0_), channel_id=1, source_target_pairs={{4,0},{5,1},{6,2},{7,3},{8,4},{9,5},{10,6},{11,7},{12,8},{13,9},{1... | collective-permute-start | bytes 1179656 | tf_op jit(solution)/shard_map/ppermute | solution.py:280
  31.7 0.7 %collective-permute-done.8.refs_4_.refs_2_ = bf16[256,768]{1,0:T(8,128)(2,1)S(1)} collective-permute-done((bf16[256,768]{1,0:T(8,128)(2,1)S(1)}, bf16[256,768]{1,0:T(8,128)(2,1)S(1)}, u32[]{:S(2)}, u32[]{:S(2)}) %collective-permute-start.8) | collective-permute-done | bytes 393248 | tf_op jit(solution)/shard_map/ppermute | solution.py:276
  32.4 3.5 %collective-permute-done.9.refs_3_.refs_5_ = bf16[256,768]{1,0:T(8,128)(2,1)S(1)} collective-permute-done((bf16[256,768]{1,0:T(8,128)(2,1)S(1)}, bf16[256,768]{1,0:T(8,128)(2,1)S(1)}, u32[]{:S(2)}, u32[]{:S(2)}) %collective-permute-start.9) | collective-permute-done | bytes 393248 | tf_op jit(solution)/shard_map/ppermute | solution.py:280
  35.9 0.0 collective-permute-start.10
  35.9 0.4 copy.16.refs_6_.refs_8_.refs_5_
  36.4 0.0 collective-permute-done.11.refs_3_
  36.4 2.4 %shard_map.40.refs_7_ = f32[8,256]{1,0:T(8,128)S(1)} custom-call(bf16[256,768]{1,0:T(8,128)(2,1)S(1)} %pad_maximum_fusion.1.refs_0_, bf16[256,768]{1,0:T(8,128)(2,1)S(1)} %pad_maximum_fusion.refs_1_.refs_0_, bf16[256,768]{1,0:T(8,128)(2,1)S(1)} %collective-permute-done.5.refs_2_, bf16[256,768]{1,0:T(8,128)(2,1)} %collective-permute-done.11.refs_3_, ...), custom_call_target="tpu_custom_call" | custom-call | tf_op jit(solution)/shard_map/pallas_call | solution.py:222
  38.8 0.0 collective-permute-done.10.refs_4_.refs_6_
  38.8 2.0 %shard_map.41.refs_9_ = f32[8,256]{1,0:T(8,128)S(1)} custom-call(bf16[256,768]{1,0:T(8,128)(2,1)S(1)} %pad_maximum_fusion.1.refs_0_, bf16[256,768]{1,0:T(8,128)(2,1)S(1)} %pad_maximum_fusion.refs_1_.refs_0_, bf16[256,768]{1,0:T(8,128)(2,1)S(1)} %collective-permute-done.8.refs_4_.refs_2_, bf16[256,768]{1,0:T(8,128)(2,1)S(1)} %collective-permute-done.9.refs_3_.refs_5_, ...), custom_call_target="tpu_custom_call" | custom-call | tf_op jit(solution)/shard_map/pallas_call | solution.py:222
  40.8 0.6 %collective-permute-done.6.refs_4_.refs_1_ = bf16[256,768]{1,0:T(8,128)(2,1)} collective-permute-done((bf16[256,768]{1,0:T(8,128)(2,1)S(1)}, bf16[256,768]{1,0:T(8,128)(2,1)}, u32[]{:S(2)}, u32[]{:S(2)}) %collective-permute-start.6) | collective-permute-done | bytes 393248 | tf_op jit(solution)/shard_map/ppermute | solution.py:276
  41.5 2.2 %collective-permute-done.7.refs_2_ = bf16[256,768]{1,0:T(8,128)(2,1)} collective-permute-done((bf16[256,768]{1,0:T(8,128)(2,1)S(1)}, bf16[256,768]{1,0:T(8,128)(2,1)}, u32[]{:S(2)}, u32[]{:S(2)}) %collective-permute-start.7) | collective-permute-done | bytes 393248 | tf_op jit(solution)/shard_map/ppermute | solution.py:280
  43.6 0.0 collective-permute-start.12
  43.6 2.2 %shard_map.42.refs_6_ = f32[8,256]{1,0:T(8,128)S(1)} custom-call(bf16[256,768]{1,0:T(8,128)(2,1)S(1)} %pad_maximum_fusion.1.refs_0_, bf16[256,768]{1,0:T(8,128)(2,1)S(1)} %pad_maximum_fusion.refs_1_.refs_0_, bf16[256,768]{1,0:T(8,128)(2,1)S(1)} %collective-permute-done.5.refs_2_, bf16[256,768]{1,0:T(8,128)(2,1)} %collective-permute-done.11.refs_3_, ...), custom_call_target="tpu_custom_call" | custom-call | tf_op jit(solution)/shard_map/pallas_call | solution.py:222
  45.8 0.0 collective-permute-done.12.refs_3_
  45.8 2.0 %shard_map.43 = f32[16,2,128]{2,1,0:T(2,128)S(1)} custom-call(bf16[256,768]{1,0:T(8,128)(2,1)S(1)} %pad_maximum_fusion.refs_1_.refs_0_, bf16[256,768]{1,0:T(8,128)(2,1)} %collective-permute-done.6.refs_4_.refs_1_, bf16[256,768]{1,0:T(8,128)(2,1)} %collective-permute-done.7.refs_2_, bf16[256,768]{1,0:T(8,128)(2,1)S(1)} %collective-permute-done.12.refs_3_, ...), custom_call_target="tpu_custom_call" | custom-call | tf_op jit(solution)/shard_map/pallas_call | solution.py:222
  47.8 10.4 %all_to_all.10.returned_ref = f32[16,2,128]{2,1,0:T(2,128)S(1)} all-to-all(f32[16,2,128]{2,1,0:T(2,128)S(1)} %shard_map.43), channel_id=1, replica_groups=mesh['grp'=2,'dev'=16] {'dev'}, dimensions={0} | all-to-all | bytes 32768 | tf_op jit(solution)/shard_map/all_to_all | solution.py:414
  58.2 1.2 %shard_map.44 = f32[1,512]{1,0:T(1,128)} custom-call(s32[1,512]{1,0:T(1,128)S(1)} %get-tuple-element.17.rank_ref, f32[16,2,128]{2,1,0:T(2,128)S(1)} %all_to_all.10.returned_ref), custom_call_target="tpu_custom_call" | custom-call | tf_op jit(solution)/shard_map/pallas_call | solution.py:415
  (31 shorter events, 0.4 us)
Async XLA Ops:
  0.0 1.1 %copy-start = (bf16[512,768]{1,0:T(8,128)(2,1)S(1)}, bf16[512,768]{1,0:T(8,128)(2,1)}, u32[]{:S(2)}) copy-start(bf16[512,768]{1,0:T(8,128)(2,1)} %rows_hbm.1) | copy-start | bytes 2359300
  1.1 0.7 %copy-start.1 = (s32[512]{0:T(512)S(1)}, s32[512]{0:T(512)}, u32[]{:S(2)}) copy-start(s32[512]{0:T(512)} %param.4) | copy-start | bytes 6148
  2.9 12.0 %collective-permute-start = (bf16[128,768]{1,0:T(8,128)(2,1)S(1)}, bf16[128,768]{1,0:T(8,128)(2,1)S(1)}, u32[]{:S(2)}, u32[]{:S(2)}) collective-permute-start(bf16[128,768]{1,0:T(8,128)(2,1)S(1)} %get-tuple-element.19.refs_2_), channel_id=1, source_target_pairs={{0,4},{1,5},{2,6},{3,7},{4,0},{5,1},{6,2},{7,3},{8,12},{9,13},{10,... | collective-permute-start | bytes 589832 | tf_op jit(solution)/shard_map/ppermute | solution.py:276
  5.9 14.0 %collective-permute-start.3 = (bf16[64,768]{1,0:T(8,128)(2,1)S(1)}, bf16[64,768]{1,0:T(8,128)(2,1)S(1)}, u32[]{:S(2)}, u32[]{:S(2)}) collective-permute-start(bf16[64,768]{1,0:T(8,128)(2,1)S(1)} %get-tuple-element.23.refs_3_), channel_id=1, source_target_pairs={{0,8},{1,9},{2,10},{3,11},{4,12},{5,13},{6,14},{7,15},{8,0},{9,1},... | collective-permute-start | bytes 294920 | tf_op jit(solution)/shard_map/ppermute | solution.py:276
  8.5 11.4 %collective-permute-start.4 = (bf16[64,768]{1,0:T(8,128)(2,1)S(1)}, bf16[64,768]{1,0:T(8,128)(2,1)S(1)}, u32[]{:S(2)}, u32[]{:S(2)}) collective-permute-start(bf16[64,768]{1,0:T(8,128)(2,1)S(1)} %get-tuple-element.24.refs_5_), channel_id=1, source_target_pairs={{0,12},{1,13},{2,14},{3,15},{4,8},{5,9},{6,10},{7,11},{8,4},{9,5},... | collective-permute-start | bytes 294920 | tf_op jit(solution)/shard_map/ppermute | solution.py:276
  8.5 18.7 %collective-permute-start.1 = (bf16[64,768]{1,0:T(8,128)(2,1)S(1)}, bf16[64,768]{1,0:T(8,128)(2,1)S(1)}, u32[]{:S(2)}, u32[]{:S(2)}) collective-permute-start(bf16[64,768]{1,0:T(8,128)(2,1)S(1)} %get-tuple-element.20.refs_4_), channel_id=1, source_target_pairs={{0,8},{1,9},{2,10},{3,11},{4,12},{5,13},{6,14},{7,15},{8,0},{9,1},... | collective-permute-start | bytes 294920 | tf_op jit(solution)/shard_map/ppermute | solution.py:276
  10.4 16.8 %collective-permute-start.2 = (bf16[64,768]{1,0:T(8,128)(2,1)S(1)}, bf16[64,768]{1,0:T(8,128)(2,1)S(1)}, u32[]{:S(2)}, u32[]{:S(2)}) collective-permute-start(bf16[64,768]{1,0:T(8,128)(2,1)S(1)} %get-tuple-element.21.refs_6_), channel_id=1, source_target_pairs={{0,12},{1,13},{2,14},{3,15},{4,8},{5,9},{6,10},{7,11},{8,4},{9,5},... | collective-permute-start | bytes 294920 | tf_op jit(solution)/shard_map/ppermute | solution.py:276
  12.4 0.7 %copy-start.2 = (s32[512]{0:T(512)S(1)}, s32[512]{0:T(512)}, u32[]{:S(2)}) copy-start(s32[512]{0:T(512)} %param.4) | copy-start | bytes 6148
  13.0 0.7 %copy-start.3 = (s32[512]{0:T(512)S(1)}, s32[512]{0:T(512)}, u32[]{:S(2)}) copy-start(s32[512]{0:T(512)} %param.5) | copy-start | bytes 6148
  14.9 13.3 %all-to-all-start = ((f32[16,8,128]{2,1,0:T(8,128)}), f32[16,8,128]{2,1,0:T(8,128)S(1)}, u32[]{:S(2)}, u32[]{:S(2)}) async-start(f32[16,8,128]{2,1,0:T(8,128)} %shard_map.38), calls=%async_computation | async-start | bytes 131072 | tf_op jit(solution)/shard_map/all_to_all | solution.py:338
  20.0 9.7 %collective-permute-start.5 = (bf16[256,768]{1,0:T(8,128)(2,1)S(1)}, bf16[256,768]{1,0:T(8,128)(2,1)S(1)}, u32[]{:S(2)}, u32[]{:S(2)}) collective-permute-start(bf16[256,768]{1,0:T(8,128)(2,1)S(1)} %pad_maximum_fusion.1.refs_0_), channel_id=1, source_target_pairs={{0,1},{1,0},{2,3},{3,2},{4,5},{5,4},{6,7},{7,6},{8,9},{9,8},{10,11... | collective-permute-start | bytes 1179656 | tf_op jit(solution)/shard_map/ppermute | solution.py:276
  20.5 11.9 %collective-permute-start.8 = (bf16[256,768]{1,0:T(8,128)(2,1)S(1)}, bf16[256,768]{1,0:T(8,128)(2,1)S(1)}, u32[]{:S(2)}, u32[]{:S(2)}) collective-permute-start(bf16[256,768]{1,0:T(8,128)(2,1)S(1)} %pad_maximum_fusion.1.refs_0_), channel_id=1, source_target_pairs={{0,2},{1,3},{2,0},{3,1},{4,6},{5,7},{6,4},{7,5},{8,10},{9,11},{10,... | collective-permute-start | bytes 1179656 | tf_op jit(solution)/shard_map/ppermute | solution.py:276
  22.2 13.7 %collective-permute-start.9 = (bf16[256,768]{1,0:T(8,128)(2,1)S(1)}, bf16[256,768]{1,0:T(8,128)(2,1)S(1)}, u32[]{:S(2)}, u32[]{:S(2)}) collective-permute-start(bf16[256,768]{1,0:T(8,128)(2,1)S(1)} %pad_maximum_fusion.1.refs_0_), channel_id=1, source_target_pairs={{0,4},{1,5},{2,6},{3,7},{4,8},{5,9},{6,10},{7,11},{8,12},{9,13},{1... | collective-permute-start | bytes 1179656 | tf_op jit(solution)/shard_map/ppermute | solution.py:280
  29.7 6.7 %collective-permute-start.11 = (bf16[256,768]{1,0:T(8,128)(2,1)S(1)}, bf16[256,768]{1,0:T(8,128)(2,1)}, u32[]{:S(2)}, u32[]{:S(2)}) collective-permute-start(bf16[256,768]{1,0:T(8,128)(2,1)S(1)} %pad_maximum_fusion.refs_1_.refs_0_), channel_id=1, source_target_pairs={{0,1},{1,0},{2,3},{3,2},{4,5},{5,4},{6,7},{7,6},{8,9},{9,8},{10,11... | collective-permute-start | bytes 1179656 | tf_op jit(solution)/shard_map/ppermute | solution.py:276
  29.8 11.6 %collective-permute-start.6 = (bf16[256,768]{1,0:T(8,128)(2,1)S(1)}, bf16[256,768]{1,0:T(8,128)(2,1)}, u32[]{:S(2)}, u32[]{:S(2)}) collective-permute-start(bf16[256,768]{1,0:T(8,128)(2,1)S(1)} %pad_maximum_fusion.refs_1_.refs_0_), channel_id=1, source_target_pairs={{0,2},{1,3},{2,0},{3,1},{4,6},{5,7},{6,4},{7,5},{8,10},{9,11},{10,... | collective-permute-start | bytes 1179656 | tf_op jit(solution)/shard_map/ppermute | solution.py:276
  30.4 13.2 %collective-permute-start.7 = (bf16[256,768]{1,0:T(8,128)(2,1)S(1)}, bf16[256,768]{1,0:T(8,128)(2,1)}, u32[]{:S(2)}, u32[]{:S(2)}) collective-permute-start(bf16[256,768]{1,0:T(8,128)(2,1)S(1)} %pad_maximum_fusion.refs_1_.refs_0_), channel_id=1, source_target_pairs={{4,0},{5,1},{6,2},{7,3},{8,4},{9,5},{10,6},{11,7},{12,8},{13,9},{1... | collective-permute-start | bytes 1179656 | tf_op jit(solution)/shard_map/ppermute | solution.py:280
  35.9 2.9 %collective-permute-start.10 = (bf16[256,768]{1,0:T(8,128)(2,1)S(1)}, bf16[256,768]{1,0:T(8,128)(2,1)}, u32[]{:S(2)}, u32[]{:S(2)}) collective-permute-start(bf16[256,768]{1,0:T(8,128)(2,1)S(1)} %collective-permute-done.9.refs_3_.refs_5_), channel_id=1, source_target_pairs={{0,1},{1,0},{2,3},{3,2},{4,5},{5,4},{6,7},{7,6},{8,9},{9,8},{10,11... | collective-permute-start | bytes 1179656 | tf_op jit(solution)/shard_map/ppermute | solution.py:276
  43.6 2.2 %collective-permute-start.12 = (bf16[256,768]{1,0:T(8,128)(2,1)}, bf16[256,768]{1,0:T(8,128)(2,1)S(1)}, u32[]{:S(2)}, u32[]{:S(2)}) collective-permute-start(bf16[256,768]{1,0:T(8,128)(2,1)} %collective-permute-done.7.refs_2_), channel_id=1, source_target_pairs={{0,1},{1,0},{2,3},{3,2},{4,5},{5,4},{6,7},{7,6},{8,9},{9,8},{10,11... | collective-permute-start | bytes 1179656 | tf_op jit(solution)/shard_map/ppermute | solution.py:276
where the time goes:
time: 60 us; the launch traced here: 59.5 us
  starting transfers between devices  23.7 us (40%)
  Pallas kernels  12.7 us (21%)
  blocking collectives  10.4 us (17%)
  waiting for transfers between devices  7.93 us (13%)
  local copies, waits for them, and re-layouts  4.12 us (7%)
    ppermute x11, starting transfers between devices, swapped(): return lax.ppermute(rows_, 'dev', [(i, i ^ bit) for i in range(peers)])  12.3 us
    all_to_all x1, blocking collectives, shards(): lax.all_to_all(outgoing, 'dev', split_axis=0, concat_axis=0, tiled=True)  10.4 us
    pallas_call x4, Pallas kernels, masses_call(): call(kernel, jax.ShapeDtypeStruct(layout or (len(SUMS), n), jnp.float32),...  8.6 us
    ppermute x2, starting transfers between devices, passed(): return lax.ppermute(rows_, 'dev', pairs)  6.34 us
    ppermute x2, waiting for transfers between devices, passed(): return lax.ppermute(rows_, 'dev', pairs)  5.65 us
    all_to_all x1, starting transfers between devices, shards(): lax.all_to_all(facts, 'dev', split_axis=0, concat_axis=0, tiled=True)  5.02 us
    unnamed x9, local copies, waits for them, and re-layouts  3.18 us
    ppermute x11, waiting for transfers between devices, swapped(): return lax.ppermute(rows_, 'dev', [(i, i ^ bit) for i in range(peers)])  1.33 us
  transfers between devices with their start and end apart: 14, of which 5 were waited for; matrix products, arithmetic and copies ran while one was open for 2% of the time, Pallas kernels for 14%

commit v1 on v0

--- a/solution.py
+++ b/solution.py
@@ -51,7 +51,8 @@
     kinds = iota((halves, n), 0) == half
     counts = jnp.dot(kinds.astype(jnp.bfloat16), earlier, preferred_element_type=jnp.float32)
     count = jnp.sum(jnp.where(kinds, counts, 0.0), axis=0, keepdims=True).astype(jnp.int32)
-    rank_ref[...] = half * per_half + count
+    rank_ref[0:1, :] = half * per_half + count
+    rank_ref[1:2, :] = place[...]
     rank = half * per_half + count
     if len(outs) > 1:
         plane = (half // 2) ^ (lax.axis_index("dev") // QUAD)
@@ -65,11 +66,13 @@
         at += out.shape[0]
 
 
-def facts_kernel(per_half, position_ref, ids_ref, rank_ref, *refs):
-    *pieces, out_ref = refs
-    n = position_ref.shape[1]
-    pick = iota((n, n), 0) == rank_ref[...]
-    where_to = position_ref[...].astype(jnp.float32)
+def facts_kernel(per_half, ids_hbm, rank_ref, *refs):
+    *pieces, out_ref, ids_ref, sem = refs
+    copy = pltpu.make_async_copy(ids_hbm, ids_ref, sem)
+    copy.start()
+    n = rank_ref.shape[1]
+    pick = iota((n, n), 0) == rank_ref[0:1, :]
+    where_to = rank_ref[1:2, :].astype(jnp.float32)
     column = jnp.sum(jnp.where(pick, where_to, 0.0), axis=1, keepdims=True)
     eye = iota((n, n), 0) == iota((n, n), 1)
     positions = jnp.sum(jnp.where(eye, column, 0.0), axis=0, keepdims=True)
@@ -87,6 +90,7 @@
             here = iota((size, n), 0) + first == iota((size, n), 1)
             total += jnp.sum(jnp.where(here, inverse, 0.0), axis=0, keepdims=True)
             k += 1
+    copy.wait()
     ids = ids_ref[...].astype(jnp.float32)
     if len(out_ref.shape) == 2:
         for k, values in enumerate((positions, total, ids, jnp.zeros_like(ids))):
@@ -229,7 +233,7 @@
 def weights_kernel(rank_ref, returned_ref, out_ref):
     peers, _, width = returned_ref.shape
     m = width // 2
-    rank = rank_ref[...]
+    rank = rank_ref[0:1, :]
     n = rank.shape[1]
     slab, upper, member = rank // width, rank // m % 2 == 1, rank % m
     plane = iota((peers, n), 0) // QUAD
@@ -290,7 +294,7 @@
     *arranged, rank = call(
         functools.partial(arrange_kernel, per_half, 2 * planes),
         [jax.ShapeDtypeStruct((size, width), embeddings.dtype) for size in pieces]
-        + [jax.ShapeDtypeStruct((1, n), jnp.int32)],
+        + [jax.ShapeDtypeStruct((2, n), jnp.int32)],
         in_specs=[in_hbm, in_hbm],
         scratch_shapes=[
             pltpu.VMEM((1, n), jnp.int32),
@@ -316,10 +320,13 @@
         lower = block[:, 0].reshape(n // 2, width)
 
     aligned = by_permutes and 2 * per_half == LANES
-    own_facts = (where_to, cluster_ids.reshape(1, n), rank, *arranged)
+    own_facts = (cluster_ids.reshape(1, n), rank, *arranged)
     facts_shape = (peers, 4 + n // LANES, LANES) if aligned else (4, n)
     facts = call(
-        functools.partial(facts_kernel, per_half), jax.ShapeDtypeStruct(facts_shape, f32)
+        functools.partial(facts_kernel, per_half),
+        jax.ShapeDtypeStruct(facts_shape, f32),
+        in_specs=[in_hbm] + [pl.BlockSpec(memory_space=pltpu.VMEM)] * (1 + len(arranged)),
+        scratch_shapes=[pltpu.VMEM((1, n), jnp.int32), pltpu.SemaphoreType.DMA],
     )(*own_facts)
     if not aligned:
         seen = jnp.pad(facts[:2], ((0, 0), (per_half, per_half)))

time: 60 us -> 59.9 us (level)
  starting transfers between devices: 23.7 us -> 24.4 us
  local copies, waits for them, and re-layouts: 4.12 us -> 3.44 us
    unnamed x9 -> x7, local copies, waits for them, and re-layouts: 3.18 us -> 2.5 us
    all_to_all x1, starting transfers between devices: 5.02 us -> 5.69 us  [shards(): lax.all_to_all(facts, 'dev', split_axis=0, concat_axis=0, tiled=True)]
where the time goes in v1:
time: 59.9 us; the launch traced here: 59.5 us
  starting transfers between devices  24.4 us (41%)
  Pallas kernels  12.7 us (21%)
  blocking collectives  10.4 us (17%)
  waiting for transfers between devices  7.93 us (13%)
  local copies, waits for them, and re-layouts  3.44 us (6%)
    ppermute x11, starting transfers between devices, swapped(): return lax.ppermute(rows_, 'dev', [(i, i ^ bit) for i in range(peers)])  12.3 us
    all_to_all x1, blocking collectives, shards(): lax.all_to_all(outgoing, 'dev', split_axis=0, concat_axis=0, tiled=True)  10.4 us
    pallas_call x4, Pallas kernels, masses_call(): call(kernel, jax.ShapeDtypeStruct(layout or (len(SUMS), n), jnp.float32),...  8.6 us
    ppermute x2, starting transfers between devices, passed(): return lax.ppermute(rows_, 'dev', pairs)  6.34 us
    all_to_all x1, starting transfers between devices, shards(): lax.all_to_all(facts, 'dev', split_axis=0, concat_axis=0, tiled=True)  5.69 us
    ppermute x2, waiting for transfers between devices, passed(): return lax.ppermute(rows_, 'dev', pairs)  5.65 us
    unnamed x7, local copies, waits for them, and re-layouts  2.5 us
    ppermute x11, waiting for transfers between devices, swapped(): return lax.ppermute(rows_, 'dev', [(i, i ^ bit) for i in range(peers)])  1.33 us
  transfers between devices with their start and end apart: 14, of which 5 were waited for; matrix products, arithmetic and copies ran while one was open for 2% of the time, Pallas kernels for 14%

profile of v1, /device:TPU:0, one launch (start us, length us, event | category | flops | bytes accessed | tf_op | source)
XLA Modules:
  0.0 59.5 jit_solution(10130441248645821450)
XLA Ops:
  0.0 0.0 copy-start
  0.0 1.1 %copy-done = bf16[512,768]{1,0:T(8,128)(2,1)S(1)} copy-done((bf16[512,768]{1,0:T(8,128)(2,1)S(1)}, bf16[512,768]{1,0:T(8,128)(2,1)}, u32[]{:S(2)}) %copy-start) | copy-done | bytes 786456
  1.1 0.0 copy-start.1
  1.1 0.7 %copy-done.1 = s32[512]{0:T(512)S(1)} copy-done((s32[512]{0:T(512)S(1)}, s32[512]{0:T(512)}, u32[]{:S(2)}) %copy-start.1) | copy-done | bytes 2072
  1.8 1.0 %shard_map.37 = (bf16[64,768]{1,0:T(8,128)(2,1)S(1)}, bf16[64,768]{1,0:T(8,128)(2,1)S(1)}, bf16[128,768]{1,0:T(8,128)(2,1)S(1)}, bf16[64,768]{1,0:T(8,128)(2,1)S...) custom-call(s32[1,512]{1,0:T(1,128)S(1)} %bitcast.27, ...), custom_call_target="tpu_custom_call" | custom-call | tf_op jit(solution)/shard_map/pallas_call | solution.py:294
  2.9 3.1 %collective-permute-start = (bf16[128,768]{1,0:T(8,128)(2,1)S(1)}, bf16[128,768]{1,0:T(8,128)(2,1)S(1)}, u32[]{:S(2)}, u32[]{:S(2)}) collective-permute-start(bf16[128,768]{1,0:T(8,128)(2,1)S(1)} %get-tuple-element.19.refs_2_), channel_id=1, source_target_pairs={{0,4},{1,5},{2,6},{3,7},{4,0},{5,1},{6,2},{7,3},{8,12},{9,13},{10,... | collective-permute-start | bytes 589832 | tf_op jit(solution)/shard_map/ppermute | solution.py:280
  5.9 2.6 %collective-permute-start.3 = (bf16[64,768]{1,0:T(8,128)(2,1)S(1)}, bf16[64,768]{1,0:T(8,128)(2,1)S(1)}, u32[]{:S(2)}, u32[]{:S(2)}) collective-permute-start(bf16[64,768]{1,0:T(8,128)(2,1)S(1)} %get-tuple-element.23.refs_3_), channel_id=1, source_target_pairs={{0,8},{1,9},{2,10},{3,11},{4,12},{5,13},{6,14},{7,15},{8,0},{9,1},... | collective-permute-start | bytes 294920 | tf_op jit(solution)/shard_map/ppermute | solution.py:280
  8.5 0.0 collective-permute-start.4
  8.5 1.9 %collective-permute-start.1 = (bf16[64,768]{1,0:T(8,128)(2,1)S(1)}, bf16[64,768]{1,0:T(8,128)(2,1)S(1)}, u32[]{:S(2)}, u32[]{:S(2)}) collective-permute-start(bf16[64,768]{1,0:T(8,128)(2,1)S(1)} %get-tuple-element.20.refs_4_), channel_id=1, source_target_pairs={{0,8},{1,9},{2,10},{3,11},{4,12},{5,13},{6,14},{7,15},{8,0},{9,1},... | collective-permute-start | bytes 294920 | tf_op jit(solution)/shard_map/ppermute | solution.py:280
  10.4 1.9 %collective-permute-start.2 = (bf16[64,768]{1,0:T(8,128)(2,1)S(1)}, bf16[64,768]{1,0:T(8,128)(2,1)S(1)}, u32[]{:S(2)}, u32[]{:S(2)}) collective-permute-start(bf16[64,768]{1,0:T(8,128)(2,1)S(1)} %get-tuple-element.21.refs_6_), channel_id=1, source_target_pairs={{0,12},{1,13},{2,14},{3,15},{4,8},{5,9},{6,10},{7,11},{8,4},{9,5},... | collective-permute-start | bytes 294920 | tf_op jit(solution)/shard_map/ppermute | solution.py:280
  12.4 0.0 copy-start.2
  12.4 0.7 %copy-done.2 = s32[512]{0:T(512)S(1)} copy-done((s32[512]{0:T(512)S(1)}, s32[512]{0:T(512)}, u32[]{:S(2)}) %copy-start.2) | copy-done | bytes 2072
  13.0 1.2 %shard_map.38 = f32[16,8,128]{2,1,0:T(8,128)} custom-call(s32[1,512]{1,0:T(1,128)S(1)} %bitcast.28, s32[2,512]{1,0:T(2,128)S(1)} %get-tuple-element.17.rank_ref, bf16[64,768]{1,0:T(8,128)(2,1)S(1)} %get-tuple-element.22.refs_0_, bf16[64,768]{1,0:T(8,128)(2,1)S(1)} %get-tuple-element.18.refs_1_, bf16[128,768]{1,0:T(8,128)(2,1)S(1)} %get-tuple-element.19.refs_2_, ...), custom_call_target="tpu_custom_call" | custom-call | tf_op jit(solution)/shard_map/pallas_call | solution.py:325
  14.2 0.0 collective-permute-done
  14.2 5.7 %all-to-all-start = ((f32[16,8,128]{2,1,0:T(8,128)}), f32[16,8,128]{2,1,0:T(8,128)S(1)}, u32[]{:S(2)}, u32[]{:S(2)}) async-start(f32[16,8,128]{2,1,0:T(8,128)} %shard_map.38), calls=%async_computation | async-start | bytes 131072 | tf_op jit(solution)/shard_map/all_to_all | solution.py:345
  20.0 0.0 collective-permute-done.3
  20.0 0.0 collective-permute-done.4
  20.0 0.5 collective-permute-start.5
  20.5 1.7 %collective-permute-start.8 = (bf16[256,768]{1,0:T(8,128)(2,1)S(1)}, bf16[256,768]{1,0:T(8,128)(2,1)S(1)}, u32[]{:S(2)}, u32[]{:S(2)}) collective-permute-start(bf16[256,768]{1,0:T(8,128)(2,1)S(1)} %pad_maximum_fusion.1.refs_0_), channel_id=1, source_target_pairs={{0,2},{1,3},{2,0},{3,1},{4,6},{5,7},{6,4},{7,5},{8,10},{9,11},{10,... | collective-permute-start | bytes 1179656 | tf_op jit(solution)/shard_map/ppermute | solution.py:280
  22.2 5.1 %collective-permute-start.9 = (bf16[256,768]{1,0:T(8,128)(2,1)S(1)}, bf16[256,768]{1,0:T(8,128)(2,1)S(1)}, u32[]{:S(2)}, u32[]{:S(2)}) collective-permute-start(bf16[256,768]{1,0:T(8,128)(2,1)S(1)} %pad_maximum_fusion.1.refs_0_), channel_id=1, source_target_pairs={{0,4},{1,5},{2,6},{3,7},{4,8},{5,9},{6,10},{7,11},{8,12},{9,13},{1... | collective-permute-start | bytes 1179656 | tf_op jit(solution)/shard_map/ppermute | solution.py:284
  27.2 0.0 collective-permute-done.1
  27.2 0.0 collective-permute-done.2
  27.3 1.0 %all-to-all-done = f32[16,8,128]{2,1,0:T(8,128)S(1)} async-done(((f32[16,8,128]{2,1,0:T(8,128)}), f32[16,8,128]{2,1,0:T(8,128)S(1)}, u32[]{:S(2)}, u32[]{:S(2)}) %all-to-all-start) | async-done | bytes 65568 | tf_op jit(solution)/shard_map/all_to_all | solution.py:345
  28.3 0.1 reshape_reshape.15
  28.6 0.1 reshape.133
  28.7 0.1 rev.32
  28.9 0.1 reshape.132
  29.0 0.6 %shard_map.39 = f32[1,2560]{1,0:T(1,128)S(1)} custom-call(s32[1,2560]{1,0:T(1,128)S(1)} %fusion.2.place_ref, f32[48,128]{1,0:T(8,128)S(1)} %fusion.1.table_ref), custom_call_target="tpu_custom_call" | custom-call | tf_op jit(solution)/shard_map/pallas_call | solution.py:376
  29.7 0.0 collective-permute-done.5.refs_2_
  29.7 0.1 collective-permute-start.11
  29.8 0.6 %collective-permute-start.6 = (bf16[256,768]{1,0:T(8,128)(2,1)S(1)}, bf16[256,768]{1,0:T(8,128)(2,1)}, u32[]{:S(2)}, u32[]{:S(2)}) collective-permute-start(bf16[256,768]{1,0:T(8,128)(2,1)S(1)} %pad_maximum_fusion.refs_1_.refs_0_), channel_id=1, source_target_pairs={{0,2},{1,3},{2,0},{3,1},{4,6},{5,7},{6,4},{7,5},{8,10},{9,11},{10,... | collective-permute-start | bytes 1179656 | tf_op jit(solution)/shard_map/ppermute | solution.py:280
  30.4 1.3 %collective-permute-start.7 = (bf16[256,768]{1,0:T(8,128)(2,1)S(1)}, bf16[256,768]{1,0:T(8,128)(2,1)}, u32[]{:S(2)}, u32[]{:S(2)}) collective-permute-start(bf16[256,768]{1,0:T(8,128)(2,1)S(1)} %pad_maximum_fusion.refs_1_.refs_0_), channel_id=1, source_target_pairs={{4,0},{5,1},{6,2},{7,3},{8,4},{9,5},{10,6},{11,7},{12,8},{13,9},{1... | collective-permute-start | bytes 1179656 | tf_op jit(solution)/shard_map/ppermute | solution.py:284
  31.7 0.7 %collective-permute-done.8.refs_4_.refs_2_ = bf16[256,768]{1,0:T(8,128)(2,1)S(1)} collective-permute-done((bf16[256,768]{1,0:T(8,128)(2,1)S(1)}, bf16[256,768]{1,0:T(8,128)(2,1)S(1)}, u32[]{:S(2)}, u32[]{:S(2)}) %collective-permute-start.8) | collective-permute-done | bytes 393248 | tf_op jit(solution)/shard_map/ppermute | solution.py:280
  32.4 3.5 %collective-permute-done.9.refs_3_.refs_5_ = bf16[256,768]{1,0:T(8,128)(2,1)S(1)} collective-permute-done((bf16[256,768]{1,0:T(8,128)(2,1)S(1)}, bf16[256,768]{1,0:T(8,128)(2,1)S(1)}, u32[]{:S(2)}, u32[]{:S(2)}) %collective-permute-start.9) | collective-permute-done | bytes 393248 | tf_op jit(solution)/shard_map/ppermute | solution.py:284
  35.9 0.0 collective-permute-start.10
  35.9 0.4 copy.16.refs_6_.refs_8_.refs_5_
  36.4 0.0 collective-permute-done.11.refs_3_
  36.4 2.4 %shard_map.40.refs_7_ = f32[8,256]{1,0:T(8,128)S(1)} custom-call(bf16[256,768]{1,0:T(8,128)(2,1)S(1)} %pad_maximum_fusion.1.refs_0_, bf16[256,768]{1,0:T(8,128)(2,1)S(1)} %pad_maximum_fusion.refs_1_.refs_0_, bf16[256,768]{1,0:T(8,128)(2,1)S(1)} %collective-permute-done.5.refs_2_, bf16[256,768]{1,0:T(8,128)(2,1)} %collective-permute-done.11.refs_3_, ...), custom_call_target="tpu_custom_call" | custom-call | tf_op jit(solution)/shard_map/pallas_call | solution.py:226
  38.8 0.0 collective-permute-done.10.refs_4_.refs_6_
  38.8 2.0 %shard_map.41.refs_9_ = f32[8,256]{1,0:T(8,128)S(1)} custom-call(bf16[256,768]{1,0:T(8,128)(2,1)S(1)} %pad_maximum_fusion.1.refs_0_, bf16[256,768]{1,0:T(8,128)(2,1)S(1)} %pad_maximum_fusion.refs_1_.refs_0_, bf16[256,768]{1,0:T(8,128)(2,1)S(1)} %collective-permute-done.8.refs_4_.refs_2_, bf16[256,768]{1,0:T(8,128)(2,1)S(1)} %collective-permute-done.9.refs_3_.refs_5_, ...), custom_call_target="tpu_custom_call" | custom-call | tf_op jit(solution)/shard_map/pallas_call | solution.py:226
  40.8 0.6 %collective-permute-done.6.refs_4_.refs_1_ = bf16[256,768]{1,0:T(8,128)(2,1)} collective-permute-done((bf16[256,768]{1,0:T(8,128)(2,1)S(1)}, bf16[256,768]{1,0:T(8,128)(2,1)}, u32[]{:S(2)}, u32[]{:S(2)}) %collective-permute-start.6) | collective-permute-done | bytes 393248 | tf_op jit(solution)/shard_map/ppermute | solution.py:280
  41.5 2.2 %collective-permute-done.7.refs_2_ = bf16[256,768]{1,0:T(8,128)(2,1)} collective-permute-done((bf16[256,768]{1,0:T(8,128)(2,1)S(1)}, bf16[256,768]{1,0:T(8,128)(2,1)}, u32[]{:S(2)}, u32[]{:S(2)}) %collective-permute-start.7) | collective-permute-done | bytes 393248 | tf_op jit(solution)/shard_map/ppermute | solution.py:284
  43.6 0.0 collective-permute-start.12
  43.6 2.2 %shard_map.42.refs_6_ = f32[8,256]{1,0:T(8,128)S(1)} custom-call(bf16[256,768]{1,0:T(8,128)(2,1)S(1)} %pad_maximum_fusion.1.refs_0_, bf16[256,768]{1,0:T(8,128)(2,1)S(1)} %pad_maximum_fusion.refs_1_.refs_0_, bf16[256,768]{1,0:T(8,128)(2,1)S(1)} %collective-permute-done.5.refs_2_, bf16[256,768]{1,0:T(8,128)(2,1)} %collective-permute-done.11.refs_3_, ...), custom_call_target="tpu_custom_call" | custom-call | tf_op jit(solution)/shard_map/pallas_call | solution.py:226
  45.8 0.0 collective-permute-done.12.refs_3_
  45.8 2.0 %shard_map.43 = f32[16,2,128]{2,1,0:T(2,128)S(1)} custom-call(bf16[256,768]{1,0:T(8,128)(2,1)S(1)} %pad_maximum_fusion.refs_1_.refs_0_, bf16[256,768]{1,0:T(8,128)(2,1)} %collective-permute-done.6.refs_4_.refs_1_, bf16[256,768]{1,0:T(8,128)(2,1)} %collective-permute-done.7.refs_2_, bf16[256,768]{1,0:T(8,128)(2,1)S(1)} %collective-permute-done.12.refs_3_, ...), custom_call_target="tpu_custom_call" | custom-call | tf_op jit(solution)/shard_map/pallas_call | solution.py:226
  47.8 10.4 %all_to_all.10.returned_ref = f32[16,2,128]{2,1,0:T(2,128)S(1)} all-to-all(f32[16,2,128]{2,1,0:T(2,128)S(1)} %shard_map.43), channel_id=1, replica_groups=mesh['grp'=2,'dev'=16] {'dev'}, dimensions={0} | all-to-all | bytes 32768 | tf_op jit(solution)/shard_map/all_to_all | solution.py:421
  58.2 1.2 %shard_map.44 = f32[1,512]{1,0:T(1,128)} custom-call(s32[2,512]{1,0:T(2,128)S(1)} %get-tuple-element.17.rank_ref, f32[16,2,128]{2,1,0:T(2,128)S(1)} %all_to_all.10.returned_ref), custom_call_target="tpu_custom_call" | custom-call | tf_op jit(solution)/shard_map/pallas_call | solution.py:422
  (31 shorter events, 0.4 us)
Async XLA Ops:
  0.0 1.1 %copy-start = (bf16[512,768]{1,0:T(8,128)(2,1)S(1)}, bf16[512,768]{1,0:T(8,128)(2,1)}, u32[]{:S(2)}) copy-start(bf16[512,768]{1,0:T(8,128)(2,1)} %rows_hbm.1) | copy-start | bytes 2359300
  1.1 0.7 %copy-start.1 = (s32[512]{0:T(512)S(1)}, s32[512]{0:T(512)}, u32[]{:S(2)}) copy-start(s32[512]{0:T(512)} %param.4) | copy-start | bytes 6148
  2.9 11.4 %collective-permute-start = (bf16[128,768]{1,0:T(8,128)(2,1)S(1)}, bf16[128,768]{1,0:T(8,128)(2,1)S(1)}, u32[]{:S(2)}, u32[]{:S(2)}) collective-permute-start(bf16[128,768]{1,0:T(8,128)(2,1)S(1)} %get-tuple-element.19.refs_2_), channel_id=1, source_target_pairs={{0,4},{1,5},{2,6},{3,7},{4,0},{5,1},{6,2},{7,3},{8,12},{9,13},{10,... | collective-permute-start | bytes 589832 | tf_op jit(solution)/shard_map/ppermute | solution.py:280
  5.9 14.0 %collective-permute-start.3 = (bf16[64,768]{1,0:T(8,128)(2,1)S(1)}, bf16[64,768]{1,0:T(8,128)(2,1)S(1)}, u32[]{:S(2)}, u32[]{:S(2)}) collective-permute-start(bf16[64,768]{1,0:T(8,128)(2,1)S(1)} %get-tuple-element.23.refs_3_), channel_id=1, source_target_pairs={{0,8},{1,9},{2,10},{3,11},{4,12},{5,13},{6,14},{7,15},{8,0},{9,1},... | collective-permute-start | bytes 294920 | tf_op jit(solution)/shard_map/ppermute | solution.py:280
  8.5 11.4 %collective-permute-start.4 = (bf16[64,768]{1,0:T(8,128)(2,1)S(1)}, bf16[64,768]{1,0:T(8,128)(2,1)S(1)}, u32[]{:S(2)}, u32[]{:S(2)}) collective-permute-start(bf16[64,768]{1,0:T(8,128)(2,1)S(1)} %get-tuple-element.24.refs_5_), channel_id=1, source_target_pairs={{0,12},{1,13},{2,14},{3,15},{4,8},{5,9},{6,10},{7,11},{8,4},{9,5},... | collective-permute-start | bytes 294920 | tf_op jit(solution)/shard_map/ppermute | solution.py:280
  8.5 18.7 %collective-permute-start.1 = (bf16[64,768]{1,0:T(8,128)(2,1)S(1)}, bf16[64,768]{1,0:T(8,128)(2,1)S(1)}, u32[]{:S(2)}, u32[]{:S(2)}) collective-permute-start(bf16[64,768]{1,0:T(8,128)(2,1)S(1)} %get-tuple-element.20.refs_4_), channel_id=1, source_target_pairs={{0,8},{1,9},{2,10},{3,11},{4,12},{5,13},{6,14},{7,15},{8,0},{9,1},... | collective-permute-start | bytes 294920 | tf_op jit(solution)/shard_map/ppermute | solution.py:280
  10.4 16.8 %collective-permute-start.2 = (bf16[64,768]{1,0:T(8,128)(2,1)S(1)}, bf16[64,768]{1,0:T(8,128)(2,1)S(1)}, u32[]{:S(2)}, u32[]{:S(2)}) collective-permute-start(bf16[64,768]{1,0:T(8,128)(2,1)S(1)} %get-tuple-element.21.refs_6_), channel_id=1, source_target_pairs={{0,12},{1,13},{2,14},{3,15},{4,8},{5,9},{6,10},{7,11},{8,4},{9,5},... | collective-permute-start | bytes 294920 | tf_op jit(solution)/shard_map/ppermute | solution.py:280
  12.4 0.7 %copy-start.2 = (s32[512]{0:T(512)S(1)}, s32[512]{0:T(512)}, u32[]{:S(2)}) copy-start(s32[512]{0:T(512)} %param.5) | copy-start | bytes 6148
  14.2 14.0 %all-to-all-start = ((f32[16,8,128]{2,1,0:T(8,128)}), f32[16,8,128]{2,1,0:T(8,128)S(1)}, u32[]{:S(2)}, u32[]{:S(2)}) async-start(f32[16,8,128]{2,1,0:T(8,128)} %shard_map.38), calls=%async_computation | async-start | bytes 131072 | tf_op jit(solution)/shard_map/all_to_all | solution.py:345
  20.0 9.7 %collective-permute-start.5 = (bf16[256,768]{1,0:T(8,128)(2,1)S(1)}, bf16[256,768]{1,0:T(8,128)(2,1)S(1)}, u32[]{:S(2)}, u32[]{:S(2)}) collective-permute-start(bf16[256,768]{1,0:T(8,128)(2,1)S(1)} %pad_maximum_fusion.1.refs_0_), channel_id=1, source_target_pairs={{0,1},{1,0},{2,3},{3,2},{4,5},{5,4},{6,7},{7,6},{8,9},{9,8},{10,11... | collective-permute-start | bytes 1179656 | tf_op jit(solution)/shard_map/ppermute | solution.py:280
  20.5 11.9 %collective-permute-start.8 = (bf16[256,768]{1,0:T(8,128)(2,1)S(1)}, bf16[256,768]{1,0:T(8,128)(2,1)S(1)}, u32[]{:S(2)}, u32[]{:S(2)}) collective-permute-start(bf16[256,768]{1,0:T(8,128)(2,1)S(1)} %pad_maximum_fusion.1.refs_0_), channel_id=1, source_target_pairs={{0,2},{1,3},{2,0},{3,1},{4,6},{5,7},{6,4},{7,5},{8,10},{9,11},{10,... | collective-permute-start | bytes 1179656 | tf_op jit(solution)/shard_map/ppermute | solution.py:280
  22.2 13.7 %collective-permute-start.9 = (bf16[256,768]{1,0:T(8,128)(2,1)S(1)}, bf16[256,768]{1,0:T(8,128)(2,1)S(1)}, u32[]{:S(2)}, u32[]{:S(2)}) collective-permute-start(bf16[256,768]{1,0:T(8,128)(2,1)S(1)} %pad_maximum_fusion.1.refs_0_), channel_id=1, source_target_pairs={{0,4},{1,5},{2,6},{3,7},{4,8},{5,9},{6,10},{7,11},{8,12},{9,13},{1... | collective-permute-start | bytes 1179656 | tf_op jit(solution)/shard_map/ppermute | solution.py:284
  29.7 6.7 %collective-permute-start.11 = (bf16[256,768]{1,0:T(8,128)(2,1)S(1)}, bf16[256,768]{1,0:T(8,128)(2,1)}, u32[]{:S(2)}, u32[]{:S(2)}) collective-permute-start(bf16[256,768]{1,0:T(8,128)(2,1)S(1)} %pad_maximum_fusion.refs_1_.refs_0_), channel_id=1, source_target_pairs={{0,1},{1,0},{2,3},{3,2},{4,5},{5,4},{6,7},{7,6},{8,9},{9,8},{10,11... | collective-permute-start | bytes 1179656 | tf_op jit(solution)/shard_map/ppermute | solution.py:280
  29.8 11.6 %collective-permute-start.6 = (bf16[256,768]{1,0:T(8,128)(2,1)S(1)}, bf16[256,768]{1,0:T(8,128)(2,1)}, u32[]{:S(2)}, u32[]{:S(2)}) collective-permute-start(bf16[256,768]{1,0:T(8,128)(2,1)S(1)} %pad_maximum_fusion.refs_1_.refs_0_), channel_id=1, source_target_pairs={{0,2},{1,3},{2,0},{3,1},{4,6},{5,7},{6,4},{7,5},{8,10},{9,11},{10,... | collective-permute-start | bytes 1179656 | tf_op jit(solution)/shard_map/ppermute | solution.py:280
  30.4 13.2 %collective-permute-start.7 = (bf16[256,768]{1,0:T(8,128)(2,1)S(1)}, bf16[256,768]{1,0:T(8,128)(2,1)}, u32[]{:S(2)}, u32[]{:S(2)}) collective-permute-start(bf16[256,768]{1,0:T(8,128)(2,1)S(1)} %pad_maximum_fusion.refs_1_.refs_0_), channel_id=1, source_target_pairs={{4,0},{5,1},{6,2},{7,3},{8,4},{9,5},{10,6},{11,7},{12,8},{13,9},{1... | collective-permute-start | bytes 1179656 | tf_op jit(solution)/shard_map/ppermute | solution.py:284
  35.9 2.9 %collective-permute-start.10 = (bf16[256,768]{1,0:T(8,128)(2,1)S(1)}, bf16[256,768]{1,0:T(8,128)(2,1)}, u32[]{:S(2)}, u32[]{:S(2)}) collective-permute-start(bf16[256,768]{1,0:T(8,128)(2,1)S(1)} %collective-permute-done.9.refs_3_.refs_5_), channel_id=1, source_target_pairs={{0,1},{1,0},{2,3},{3,2},{4,5},{5,4},{6,7},{7,6},{8,9},{9,8},{10,11... | collective-permute-start | bytes 1179656 | tf_op jit(solution)/shard_map/ppermute | solution.py:280
  43.6 2.2 %collective-permute-start.12 = (bf16[256,768]{1,0:T(8,128)(2,1)}, bf16[256,768]{1,0:T(8,128)(2,1)S(1)}, u32[]{:S(2)}, u32[]{:S(2)}) collective-permute-start(bf16[256,768]{1,0:T(8,128)(2,1)} %collective-permute-done.7.refs_2_), channel_id=1, source_target_pairs={{0,1},{1,0},{2,3},{3,2},{4,5},{5,4},{6,7},{7,6},{8,9},{9,8},{10,11... | collective-permute-start | bytes 1179656 | tf_op jit(solution)/shard_map/ppermute | solution.py:280

commit v2 on v0

--- a/solution.py
+++ b/solution.py
@@ -13,7 +13,7 @@
 SIMILARITY_CUTOFF = 0.9
 SOFTMAX_HEAT = 0.02
 SCALE = math.log2(math.e) / SOFTMAX_HEAT
-SHIFT = SIMILARITY_CUTOFF * SCALE
+FACTOR = math.exp(-SIMILARITY_CUTOFF / SOFTMAX_HEAT)
 QUAD = 4
 CHUNK = 256
 LANES = 128
@@ -144,7 +144,7 @@
         at, to = NAMES.index(down) * n, NAMES.index(across) * n
         scale = self.columns[at : at + n, 0:1]
         label = self.columns[at : at + n, 1:2]
-        power = products * scale * self.rows[0:1, to : to + n] - SHIFT
+        power = products * scale * self.rows[0:1, to : to + n]
         mask = label == self.rows[1:2, to : to + n]
         if down == across:
             mask &= iota((n, n), 0) != iota((n, n), 1)
@@ -247,7 +247,7 @@
 
     mass = chosen(0, slab, jnp.where(upper, m + member, member))
     mass += chosen(1, jnp.where(upper, slab + 1, slab - 1), jnp.where(upper, member, m + member))
-    out_ref[...] = 1.0 / (1.0 + mass)
+    out_ref[...] = 1.0 / (1.0 + mass * FACTOR)
 
 
 def xor_order(array, axis, bits):

time: 60 us -> 59.9 us (level)
  no operation moved by 1% of the time
where the time goes in v2:
time: 59.9 us; the launch traced here: 59.4 us
  starting transfers between devices  23.7 us (40%)
  Pallas kernels  12.6 us (21%)
  blocking collectives  10.4 us (17%)
  waiting for transfers between devices  7.96 us (13%)
  local copies, waits for them, and re-layouts  4.12 us (7%)
    ppermute x11, starting transfers between devices, swapped(): return lax.ppermute(rows_, 'dev', [(i, i ^ bit) for i in range(peers)])  12.3 us
    all_to_all x1, blocking collectives, shards(): lax.all_to_all(outgoing, 'dev', split_axis=0, concat_axis=0, tiled=True)  10.4 us
    pallas_call x4, Pallas kernels, masses_call(): call(kernel, jax.ShapeDtypeStruct(layout or (len(SUMS), n), jnp.float32),...  8.53 us
    ppermute x2, starting transfers between devices, passed(): return lax.ppermute(rows_, 'dev', pairs)  6.34 us
    ppermute x2, waiting for transfers between devices, passed(): return lax.ppermute(rows_, 'dev', pairs)  5.65 us
    all_to_all x1, starting transfers between devices, shards(): lax.all_to_all(facts, 'dev', split_axis=0, concat_axis=0, tiled=True)  5.02 us
    unnamed x9, local copies, waits for them, and re-layouts  3.18 us
    ppermute x11, waiting for transfers between devices, swapped(): return lax.ppermute(rows_, 'dev', [(i, i ^ bit) for i in range(peers)])  1.36 us
  transfers between devices with their start and end apart: 14, of which 5 were waited for; matrix products, arithmetic and copies ran while one was open for 2% of the time, Pallas kernels for 14%

profile of v2, /device:TPU:0, one launch (start us, length us, event | category | flops | bytes accessed | tf_op | source)
XLA Modules:
  0.0 59.4 jit_solution(11758553260585583781)
XLA Ops:
  0.0 0.0 copy-start
  0.0 1.1 %copy-done = bf16[512,768]{1,0:T(8,128)(2,1)S(1)} copy-done((bf16[512,768]{1,0:T(8,128)(2,1)S(1)}, bf16[512,768]{1,0:T(8,128)(2,1)}, u32[]{:S(2)}) %copy-start) | copy-done | bytes 786456
  1.1 0.0 copy-start.1
  1.1 0.7 %copy-done.1 = s32[512]{0:T(512)S(1)} copy-done((s32[512]{0:T(512)S(1)}, s32[512]{0:T(512)}, u32[]{:S(2)}) %copy-start.1) | copy-done | bytes 2072
  1.8 1.0 %shard_map.37 = (bf16[64,768]{1,0:T(8,128)(2,1)S(1)}, bf16[64,768]{1,0:T(8,128)(2,1)S(1)}, bf16[128,768]{1,0:T(8,128)(2,1)S(1)}, bf16[64,768]{1,0:T(8,128)(2,1)S...) custom-call(s32[1,512]{1,0:T(1,128)S(1)} %bitcast.27, ...), custom_call_target="tpu_custom_call" | custom-call | tf_op jit(solution)/shard_map/pallas_call | solution.py:290
  2.9 3.1 %collective-permute-start = (bf16[128,768]{1,0:T(8,128)(2,1)S(1)}, bf16[128,768]{1,0:T(8,128)(2,1)S(1)}, u32[]{:S(2)}, u32[]{:S(2)}) collective-permute-start(bf16[128,768]{1,0:T(8,128)(2,1)S(1)} %get-tuple-element.19.refs_2_), channel_id=1, source_target_pairs={{0,4},{1,5},{2,6},{3,7},{4,0},{5,1},{6,2},{7,3},{8,12},{9,13},{10,... | collective-permute-start | bytes 589832 | tf_op jit(solution)/shard_map/ppermute | solution.py:276
  5.9 2.6 %collective-permute-start.3 = (bf16[64,768]{1,0:T(8,128)(2,1)S(1)}, bf16[64,768]{1,0:T(8,128)(2,1)S(1)}, u32[]{:S(2)}, u32[]{:S(2)}) collective-permute-start(bf16[64,768]{1,0:T(8,128)(2,1)S(1)} %get-tuple-element.23.refs_3_), channel_id=1, source_target_pairs={{0,8},{1,9},{2,10},{3,11},{4,12},{5,13},{6,14},{7,15},{8,0},{9,1},... | collective-permute-start | bytes 294920 | tf_op jit(solution)/shard_map/ppermute | solution.py:276
  8.5 0.0 collective-permute-start.4
  8.5 1.9 %collective-permute-start.1 = (bf16[64,768]{1,0:T(8,128)(2,1)S(1)}, bf16[64,768]{1,0:T(8,128)(2,1)S(1)}, u32[]{:S(2)}, u32[]{:S(2)}) collective-permute-start(bf16[64,768]{1,0:T(8,128)(2,1)S(1)} %get-tuple-element.20.refs_4_), channel_id=1, source_target_pairs={{0,8},{1,9},{2,10},{3,11},{4,12},{5,13},{6,14},{7,15},{8,0},{9,1},... | collective-permute-start | bytes 294920 | tf_op jit(solution)/shard_map/ppermute | solution.py:276
  10.4 1.9 %collective-permute-start.2 = (bf16[64,768]{1,0:T(8,128)(2,1)S(1)}, bf16[64,768]{1,0:T(8,128)(2,1)S(1)}, u32[]{:S(2)}, u32[]{:S(2)}) collective-permute-start(bf16[64,768]{1,0:T(8,128)(2,1)S(1)} %get-tuple-element.21.refs_6_), channel_id=1, source_target_pairs={{0,12},{1,13},{2,14},{3,15},{4,8},{5,9},{6,10},{7,11},{8,4},{9,5},... | collective-permute-start | bytes 294920 | tf_op jit(solution)/shard_map/ppermute | solution.py:276
  12.4 0.0 copy-start.2
  12.4 0.7 %copy-done.2 = s32[512]{0:T(512)S(1)} copy-done((s32[512]{0:T(512)S(1)}, s32[512]{0:T(512)}, u32[]{:S(2)}) %copy-start.2) | copy-done | bytes 2072
  13.0 0.0 copy-start.3
  13.0 0.7 %copy-done.3 = s32[512]{0:T(512)S(1)} copy-done((s32[512]{0:T(512)S(1)}, s32[512]{0:T(512)}, u32[]{:S(2)}) %copy-start.3) | copy-done | bytes 2072
  13.7 1.2 %shard_map.38 = f32[16,8,128]{2,1,0:T(8,128)} custom-call(s32[1,512]{1,0:T(1,128)S(1)} %bitcast.28, s32[1,512]{1,0:T(1,128)S(1)} %bitcast.29, s32[1,512]{1,0:T(1,128)S(1)} %get-tuple-element.17.rank_ref, bf16[64,768]{1,0:T(8,128)(2,1)S(1)} %get-tuple-element.22.refs_0_, bf16[64,768]{1,0:T(8,128)(2,1)S(1)} %get-tuple-element.18.refs_1_, ...), custom_call_target="tpu_custom_call" | custom-call | tf_op jit(solution)/shard_map/pallas_call | solution.py:321
  14.9 0.0 collective-permute-done
  14.9 5.0 %all-to-all-start = ((f32[16,8,128]{2,1,0:T(8,128)}), f32[16,8,128]{2,1,0:T(8,128)S(1)}, u32[]{:S(2)}, u32[]{:S(2)}) async-start(f32[16,8,128]{2,1,0:T(8,128)} %shard_map.38), calls=%async_computation | async-start | bytes 131072 | tf_op jit(solution)/shard_map/all_to_all | solution.py:338
  20.0 0.0 collective-permute-done.3
  20.0 0.0 collective-permute-done.4
  20.0 0.5 collective-permute-start.5
  20.5 1.7 %collective-permute-start.8 = (bf16[256,768]{1,0:T(8,128)(2,1)S(1)}, bf16[256,768]{1,0:T(8,128)(2,1)S(1)}, u32[]{:S(2)}, u32[]{:S(2)}) collective-permute-start(bf16[256,768]{1,0:T(8,128)(2,1)S(1)} %pad_maximum_fusion.1.refs_0_), channel_id=1, source_target_pairs={{0,2},{1,3},{2,0},{3,1},{4,6},{5,7},{6,4},{7,5},{8,10},{9,11},{10,... | collective-permute-start | bytes 1179656 | tf_op jit(solution)/shard_map/ppermute | solution.py:276
  22.2 5.1 %collective-permute-start.9 = (bf16[256,768]{1,0:T(8,128)(2,1)S(1)}, bf16[256,768]{1,0:T(8,128)(2,1)S(1)}, u32[]{:S(2)}, u32[]{:S(2)}) collective-permute-start(bf16[256,768]{1,0:T(8,128)(2,1)S(1)} %pad_maximum_fusion.1.refs_0_), channel_id=1, source_target_pairs={{0,4},{1,5},{2,6},{3,7},{4,8},{5,9},{6,10},{7,11},{8,12},{9,13},{1... | collective-permute-start | bytes 1179656 | tf_op jit(solution)/shard_map/ppermute | solution.py:280
  27.2 0.0 collective-permute-done.1
  27.2 0.0 collective-permute-done.2
  27.3 1.0 %all-to-all-done = f32[16,8,128]{2,1,0:T(8,128)S(1)} async-done(((f32[16,8,128]{2,1,0:T(8,128)}), f32[16,8,128]{2,1,0:T(8,128)S(1)}, u32[]{:S(2)}, u32[]{:S(2)}) %all-to-all-start) | async-done | bytes 65568 | tf_op jit(solution)/shard_map/all_to_all | solution.py:338
  28.3 0.1 reshape_reshape.15
  28.6 0.1 reshape.133
  28.7 0.1 rev.32
  28.9 0.1 reshape.132
  29.0 0.6 %shard_map.39 = f32[1,2560]{1,0:T(1,128)S(1)} custom-call(s32[1,2560]{1,0:T(1,128)S(1)} %fusion.2.place_ref, f32[48,128]{1,0:T(8,128)S(1)} %fusion.1.table_ref), custom_call_target="tpu_custom_call" | custom-call | tf_op jit(solution)/shard_map/pallas_call | solution.py:369
  29.7 0.0 collective-permute-done.5.refs_2_
  29.7 0.1 collective-permute-start.11
  29.8 0.6 %collective-permute-start.6 = (bf16[256,768]{1,0:T(8,128)(2,1)S(1)}, bf16[256,768]{1,0:T(8,128)(2,1)}, u32[]{:S(2)}, u32[]{:S(2)}) collective-permute-start(bf16[256,768]{1,0:T(8,128)(2,1)S(1)} %pad_maximum_fusion.refs_1_.refs_0_), channel_id=1, source_target_pairs={{0,2},{1,3},{2,0},{3,1},{4,6},{5,7},{6,4},{7,5},{8,10},{9,11},{10,... | collective-permute-start | bytes 1179656 | tf_op jit(solution)/shard_map/ppermute | solution.py:276
  30.4 1.3 %collective-permute-start.7 = (bf16[256,768]{1,0:T(8,128)(2,1)S(1)}, bf16[256,768]{1,0:T(8,128)(2,1)}, u32[]{:S(2)}, u32[]{:S(2)}) collective-permute-start(bf16[256,768]{1,0:T(8,128)(2,1)S(1)} %pad_maximum_fusion.refs_1_.refs_0_), channel_id=1, source_target_pairs={{4,0},{5,1},{6,2},{7,3},{8,4},{9,5},{10,6},{11,7},{12,8},{13,9},{1... | collective-permute-start | bytes 1179656 | tf_op jit(solution)/shard_map/ppermute | solution.py:280
  31.7 0.7 %collective-permute-done.8.refs_4_.refs_2_ = bf16[256,768]{1,0:T(8,128)(2,1)S(1)} collective-permute-done((bf16[256,768]{1,0:T(8,128)(2,1)S(1)}, bf16[256,768]{1,0:T(8,128)(2,1)S(1)}, u32[]{:S(2)}, u32[]{:S(2)}) %collective-permute-start.8) | collective-permute-done | bytes 393248 | tf_op jit(solution)/shard_map/ppermute | solution.py:276
  32.4 3.5 %collective-permute-done.9.refs_3_.refs_5_ = bf16[256,768]{1,0:T(8,128)(2,1)S(1)} collective-permute-done((bf16[256,768]{1,0:T(8,128)(2,1)S(1)}, bf16[256,768]{1,0:T(8,128)(2,1)S(1)}, u32[]{:S(2)}, u32[]{:S(2)}) %collective-permute-start.9) | collective-permute-done | bytes 393248 | tf_op jit(solution)/shard_map/ppermute | solution.py:280
  35.9 0.0 collective-permute-start.10
  35.9 0.4 copy.16.refs_6_.refs_8_.refs_5_
  36.4 0.0 collective-permute-done.11.refs_3_
  36.4 2.4 %shard_map.40.refs_7_ = f32[8,256]{1,0:T(8,128)S(1)} custom-call(bf16[256,768]{1,0:T(8,128)(2,1)S(1)} %pad_maximum_fusion.1.refs_0_, bf16[256,768]{1,0:T(8,128)(2,1)S(1)} %pad_maximum_fusion.refs_1_.refs_0_, bf16[256,768]{1,0:T(8,128)(2,1)S(1)} %collective-permute-done.5.refs_2_, bf16[256,768]{1,0:T(8,128)(2,1)} %collective-permute-done.11.refs_3_, ...), custom_call_target="tpu_custom_call" | custom-call | tf_op jit(solution)/shard_map/pallas_call | solution.py:222
  38.8 0.0 collective-permute-done.10.refs_4_.refs_6_
  38.8 2.0 %shard_map.41.refs_9_ = f32[8,256]{1,0:T(8,128)S(1)} custom-call(bf16[256,768]{1,0:T(8,128)(2,1)S(1)} %pad_maximum_fusion.1.refs_0_, bf16[256,768]{1,0:T(8,128)(2,1)S(1)} %pad_maximum_fusion.refs_1_.refs_0_, bf16[256,768]{1,0:T(8,128)(2,1)S(1)} %collective-permute-done.8.refs_4_.refs_2_, bf16[256,768]{1,0:T(8,128)(2,1)S(1)} %collective-permute-done.9.refs_3_.refs_5_, ...), custom_call_target="tpu_custom_call" | custom-call | tf_op jit(solution)/shard_map/pallas_call | solution.py:222
  40.8 0.7 %collective-permute-done.6.refs_4_.refs_1_ = bf16[256,768]{1,0:T(8,128)(2,1)} collective-permute-done((bf16[256,768]{1,0:T(8,128)(2,1)S(1)}, bf16[256,768]{1,0:T(8,128)(2,1)}, u32[]{:S(2)}, u32[]{:S(2)}) %collective-permute-start.6) | collective-permute-done | bytes 393248 | tf_op jit(solution)/shard_map/ppermute | solution.py:276
  41.5 2.2 %collective-permute-done.7.refs_2_ = bf16[256,768]{1,0:T(8,128)(2,1)} collective-permute-done((bf16[256,768]{1,0:T(8,128)(2,1)S(1)}, bf16[256,768]{1,0:T(8,128)(2,1)}, u32[]{:S(2)}, u32[]{:S(2)}) %collective-permute-start.7) | collective-permute-done | bytes 393248 | tf_op jit(solution)/shard_map/ppermute | solution.py:280
  43.6 0.0 collective-permute-start.12
  43.6 2.2 %shard_map.42.refs_6_ = f32[8,256]{1,0:T(8,128)S(1)} custom-call(bf16[256,768]{1,0:T(8,128)(2,1)S(1)} %pad_maximum_fusion.1.refs_0_, bf16[256,768]{1,0:T(8,128)(2,1)S(1)} %pad_maximum_fusion.refs_1_.refs_0_, bf16[256,768]{1,0:T(8,128)(2,1)S(1)} %collective-permute-done.5.refs_2_, bf16[256,768]{1,0:T(8,128)(2,1)} %collective-permute-done.11.refs_3_, ...), custom_call_target="tpu_custom_call" | custom-call | tf_op jit(solution)/shard_map/pallas_call | solution.py:222
  45.8 0.0 collective-permute-done.12.refs_3_
  45.8 2.0 %shard_map.43 = f32[16,2,128]{2,1,0:T(2,128)S(1)} custom-call(bf16[256,768]{1,0:T(8,128)(2,1)S(1)} %pad_maximum_fusion.refs_1_.refs_0_, bf16[256,768]{1,0:T(8,128)(2,1)} %collective-permute-done.6.refs_4_.refs_1_, bf16[256,768]{1,0:T(8,128)(2,1)} %collective-permute-done.7.refs_2_, bf16[256,768]{1,0:T(8,128)(2,1)S(1)} %collective-permute-done.12.refs_3_, ...), custom_call_target="tpu_custom_call" | custom-call | tf_op jit(solution)/shard_map/pallas_call | solution.py:222
  47.8 10.4 %all_to_all.10.returned_ref = f32[16,2,128]{2,1,0:T(2,128)S(1)} all-to-all(f32[16,2,128]{2,1,0:T(2,128)S(1)} %shard_map.43), channel_id=1, replica_groups=mesh['grp'=2,'dev'=16] {'dev'}, dimensions={0} | all-to-all | bytes 32768 | tf_op jit(solution)/shard_map/all_to_all | solution.py:414
  58.2 1.2 %shard_map.44 = f32[1,512]{1,0:T(1,128)} custom-call(s32[1,512]{1,0:T(1,128)S(1)} %get-tuple-element.17.rank_ref, f32[16,2,128]{2,1,0:T(2,128)S(1)} %all_to_all.10.returned_ref), custom_call_target="tpu_custom_call" | custom-call | tf_op jit(solution)/shard_map/pallas_call | solution.py:415
  (31 shorter events, 0.4 us)
Async XLA Ops:
  0.0 1.1 %copy-start = (bf16[512,768]{1,0:T(8,128)(2,1)S(1)}, bf16[512,768]{1,0:T(8,128)(2,1)}, u32[]{:S(2)}) copy-start(bf16[512,768]{1,0:T(8,128)(2,1)} %rows_hbm.1) | copy-start | bytes 2359300
  1.1 0.7 %copy-start.1 = (s32[512]{0:T(512)S(1)}, s32[512]{0:T(512)}, u32[]{:S(2)}) copy-start(s32[512]{0:T(512)} %param.4) | copy-start | bytes 6148
  2.9 12.0 %collective-permute-start = (bf16[128,768]{1,0:T(8,128)(2,1)S(1)}, bf16[128,768]{1,0:T(8,128)(2,1)S(1)}, u32[]{:S(2)}, u32[]{:S(2)}) collective-permute-start(bf16[128,768]{1,0:T(8,128)(2,1)S(1)} %get-tuple-element.19.refs_2_), channel_id=1, source_target_pairs={{0,4},{1,5},{2,6},{3,7},{4,0},{5,1},{6,2},{7,3},{8,12},{9,13},{10,... | collective-permute-start | bytes 589832 | tf_op jit(solution)/shard_map/ppermute | solution.py:276
  5.9 14.0 %collective-permute-start.3 = (bf16[64,768]{1,0:T(8,128)(2,1)S(1)}, bf16[64,768]{1,0:T(8,128)(2,1)S(1)}, u32[]{:S(2)}, u32[]{:S(2)}) collective-permute-start(bf16[64,768]{1,0:T(8,128)(2,1)S(1)} %get-tuple-element.23.refs_3_), channel_id=1, source_target_pairs={{0,8},{1,9},{2,10},{3,11},{4,12},{5,13},{6,14},{7,15},{8,0},{9,1},... | collective-permute-start | bytes 294920 | tf_op jit(solution)/shard_map/ppermute | solution.py:276
  8.5 11.4 %collective-permute-start.4 = (bf16[64,768]{1,0:T(8,128)(2,1)S(1)}, bf16[64,768]{1,0:T(8,128)(2,1)S(1)}, u32[]{:S(2)}, u32[]{:S(2)}) collective-permute-start(bf16[64,768]{1,0:T(8,128)(2,1)S(1)} %get-tuple-element.24.refs_5_), channel_id=1, source_target_pairs={{0,12},{1,13},{2,14},{3,15},{4,8},{5,9},{6,10},{7,11},{8,4},{9,5},... | collective-permute-start | bytes 294920 | tf_op jit(solution)/shard_map/ppermute | solution.py:276
  8.5 18.7 %collective-permute-start.1 = (bf16[64,768]{1,0:T(8,128)(2,1)S(1)}, bf16[64,768]{1,0:T(8,128)(2,1)S(1)}, u32[]{:S(2)}, u32[]{:S(2)}) collective-permute-start(bf16[64,768]{1,0:T(8,128)(2,1)S(1)} %get-tuple-element.20.refs_4_), channel_id=1, source_target_pairs={{0,8},{1,9},{2,10},{3,11},{4,12},{5,13},{6,14},{7,15},{8,0},{9,1},... | collective-permute-start | bytes 294920 | tf_op jit(solution)/shard_map/ppermute | solution.py:276
  10.4 16.8 %collective-permute-start.2 = (bf16[64,768]{1,0:T(8,128)(2,1)S(1)}, bf16[64,768]{1,0:T(8,128)(2,1)S(1)}, u32[]{:S(2)}, u32[]{:S(2)}) collective-permute-start(bf16[64,768]{1,0:T(8,128)(2,1)S(1)} %get-tuple-element.21.refs_6_), channel_id=1, source_target_pairs={{0,12},{1,13},{2,14},{3,15},{4,8},{5,9},{6,10},{7,11},{8,4},{9,5},... | collective-permute-start | bytes 294920 | tf_op jit(solution)/shard_map/ppermute | solution.py:276
  12.4 0.7 %copy-start.2 = (s32[512]{0:T(512)S(1)}, s32[512]{0:T(512)}, u32[]{:S(2)}) copy-start(s32[512]{0:T(512)} %param.4) | copy-start | bytes 6148
  13.0 0.7 %copy-start.3 = (s32[512]{0:T(512)S(1)}, s32[512]{0:T(512)}, u32[]{:S(2)}) copy-start(s32[512]{0:T(512)} %param.5) | copy-start | bytes 6148
  14.9 13.3 %all-to-all-start = ((f32[16,8,128]{2,1,0:T(8,128)}), f32[16,8,128]{2,1,0:T(8,128)S(1)}, u32[]{:S(2)}, u32[]{:S(2)}) async-start(f32[16,8,128]{2,1,0:T(8,128)} %shard_map.38), calls=%async_computation | async-start | bytes 131072 | tf_op jit(solution)/shard_map/all_to_all | solution.py:338
  20.0 9.7 %collective-permute-start.5 = (bf16[256,768]{1,0:T(8,128)(2,1)S(1)}, bf16[256,768]{1,0:T(8,128)(2,1)S(1)}, u32[]{:S(2)}, u32[]{:S(2)}) collective-permute-start(bf16[256,768]{1,0:T(8,128)(2,1)S(1)} %pad_maximum_fusion.1.refs_0_), channel_id=1, source_target_pairs={{0,1},{1,0},{2,3},{3,2},{4,5},{5,4},{6,7},{7,6},{8,9},{9,8},{10,11... | collective-permute-start | bytes 1179656 | tf_op jit(solution)/shard_map/ppermute | solution.py:276
  20.5 11.9 %collective-permute-start.8 = (bf16[256,768]{1,0:T(8,128)(2,1)S(1)}, bf16[256,768]{1,0:T(8,128)(2,1)S(1)}, u32[]{:S(2)}, u32[]{:S(2)}) collective-permute-start(bf16[256,768]{1,0:T(8,128)(2,1)S(1)} %pad_maximum_fusion.1.refs_0_), channel_id=1, source_target_pairs={{0,2},{1,3},{2,0},{3,1},{4,6},{5,7},{6,4},{7,5},{8,10},{9,11},{10,... | collective-permute-start | bytes 1179656 | tf_op jit(solution)/shard_map/ppermute | solution.py:276
  22.2 13.7 %collective-permute-start.9 = (bf16[256,768]{1,0:T(8,128)(2,1)S(1)}, bf16[256,768]{1,0:T(8,128)(2,1)S(1)}, u32[]{:S(2)}, u32[]{:S(2)}) collective-permute-start(bf16[256,768]{1,0:T(8,128)(2,1)S(1)} %pad_maximum_fusion.1.refs_0_), channel_id=1, source_target_pairs={{0,4},{1,5},{2,6},{3,7},{4,8},{5,9},{6,10},{7,11},{8,12},{9,13},{1... | collective-permute-start | bytes 1179656 | tf_op jit(solution)/shard_map/ppermute | solution.py:280
  29.7 6.7 %collective-permute-start.11 = (bf16[256,768]{1,0:T(8,128)(2,1)S(1)}, bf16[256,768]{1,0:T(8,128)(2,1)}, u32[]{:S(2)}, u32[]{:S(2)}) collective-permute-start(bf16[256,768]{1,0:T(8,128)(2,1)S(1)} %pad_maximum_fusion.refs_1_.refs_0_), channel_id=1, source_target_pairs={{0,1},{1,0},{2,3},{3,2},{4,5},{5,4},{6,7},{7,6},{8,9},{9,8},{10,11... | collective-permute-start | bytes 1179656 | tf_op jit(solution)/shard_map/ppermute | solution.py:276
  29.8 11.6 %collective-permute-start.6 = (bf16[256,768]{1,0:T(8,128)(2,1)S(1)}, bf16[256,768]{1,0:T(8,128)(2,1)}, u32[]{:S(2)}, u32[]{:S(2)}) collective-permute-start(bf16[256,768]{1,0:T(8,128)(2,1)S(1)} %pad_maximum_fusion.refs_1_.refs_0_), channel_id=1, source_target_pairs={{0,2},{1,3},{2,0},{3,1},{4,6},{5,7},{6,4},{7,5},{8,10},{9,11},{10,... | collective-permute-start | bytes 1179656 | tf_op jit(solution)/shard_map/ppermute | solution.py:276
  30.4 13.2 %collective-permute-start.7 = (bf16[256,768]{1,0:T(8,128)(2,1)S(1)}, bf16[256,768]{1,0:T(8,128)(2,1)}, u32[]{:S(2)}, u32[]{:S(2)}) collective-permute-start(bf16[256,768]{1,0:T(8,128)(2,1)S(1)} %pad_maximum_fusion.refs_1_.refs_0_), channel_id=1, source_target_pairs={{4,0},{5,1},{6,2},{7,3},{8,4},{9,5},{10,6},{11,7},{12,8},{13,9},{1... | collective-permute-start | bytes 1179656 | tf_op jit(solution)/shard_map/ppermute | solution.py:280
  35.9 2.9 %collective-permute-start.10 = (bf16[256,768]{1,0:T(8,128)(2,1)S(1)}, bf16[256,768]{1,0:T(8,128)(2,1)}, u32[]{:S(2)}, u32[]{:S(2)}) collective-permute-start(bf16[256,768]{1,0:T(8,128)(2,1)S(1)} %collective-permute-done.9.refs_3_.refs_5_), channel_id=1, source_target_pairs={{0,1},{1,0},{2,3},{3,2},{4,5},{5,4},{6,7},{7,6},{8,9},{9,8},{10,11... | collective-permute-start | bytes 1179656 | tf_op jit(solution)/shard_map/ppermute | solution.py:276
  43.6 2.2 %collective-permute-start.12 = (bf16[256,768]{1,0:T(8,128)(2,1)}, bf16[256,768]{1,0:T(8,128)(2,1)S(1)}, u32[]{:S(2)}, u32[]{:S(2)}) collective-permute-start(bf16[256,768]{1,0:T(8,128)(2,1)} %collective-permute-done.7.refs_2_), channel_id=1, source_target_pairs={{0,1},{1,0},{2,3},{3,2},{4,5},{5,4},{6,7},{7,6},{8,9},{9,8},{10,11... | collective-permute-start | bytes 1179656 | tf_op jit(solution)/shard_map/ppermute | solution.py:276

commit v3 on v0

--- a/solution.py
+++ b/solution.py
@@ -383,14 +383,15 @@
         + [("b0l", "b0l"), ("b0h", "b0l"), ("b1h", "b0l"), ("b2h", "b0l")]
         + [("b1l", "b0h"), ("b1l", "b0l"), ("b1l", "b2h")]
     )
-    arrays["u1"] = swapped(after_all(arrays['u'], arrays["b2h"]), 1)
-    masses = masses_after([(u, b) for u in ("u", "u1") for b in ("b0h", "b0l", "b2h")], masses)
-    arrays["l1"] = swapped(after_all(arrays["l"], masses, arrays["b2l"]), 1)
+    masses = masses_after([("u", "b0h"), ("u", "b0l"), ("u", "b2h")], masses)
+    arrays["u1"] = swapped(after_all(arrays["u"], arrays["l"]), 1)
+    arrays["l1"] = swapped(after_all(arrays["l"], masses), 1)
     masses = masses_after(
-        [("b2l", "b0h"), ("b2l", "b0l"), ("b1h", "b2l"), ("b1l", "b2l"), ("u", "b2l"), ("u1", "b2l")],
+        [("b2l", "b0h"), ("b2l", "b0l"), ("b1h", "b2l"), ("b1l", "b2l")]
+        + [("u", "b2l"), ("l", "b0l"), ("l", "b2l")],
         masses,
     )
-    last = [("l", "b0l"), ("l", "b2l"), ("l1", "b0l"), ("l1", "b2l")]
+    last = [("u1", b) for b in ("b0h", "b0l", "b2h", "b2l")] + [("l1", "b0l"), ("l1", "b2l")]
     if by_permutes:
         outgoing = masses_call(last, arrays, rows, columns, masses, (peers, 2, 2 * per_half))
     else:

time: 60 us -> 59.9 us (level)
  Pallas kernels: 12.7 us -> 10.4 us
  starting transfers between devices: 23.7 us -> 25 us
  blocking collectives: 10.4 us -> 11.1 us
    pallas_call x4, Pallas kernels: 8.6 us -> 6.3 us  [masses_call(): call(kernel, jax.ShapeDtypeStruct(layout or (len(SUMS), n), jnp.float32),...]
    ppermute x2, waiting for transfers between devices: 5.65 us -> 7.89 us  [passed(): return lax.ppermute(rows_, 'dev', pairs)]
    ppermute x11, waiting for transfers between devices: 1.33 us -> 0.14 us  [swapped(): return lax.ppermute(rows_, 'dev', [(i, i ^ bit) for i in range(peers)])]
    ppermute x2, starting transfers between devices: 6.34 us -> 7.09 us  [passed(): return lax.ppermute(rows_, 'dev', pairs)]
    all_to_all x1, blocking collectives: 10.4 us -> 11.1 us  [shards(): lax.all_to_all(outgoing, 'dev', split_axis=0, concat_axis=0, tiled=True)]
    all_to_all x1, waiting for transfers between devices: 0.96 us -> 0.25 us  [shards(): lax.all_to_all(facts, 'dev', split_axis=0, concat_axis=0, tiled=True)]
  transfers between devices with their start and end apart: 14 -> 14, of which waited for: 5 -> 4; matrix products, arithmetic and copies ran while one was open for 2% -> 2% of each run, Pallas kernels for 14% -> 12%
where the time goes in v3:
time: 59.9 us; the launch traced here: 59.5 us
  starting transfers between devices  25 us (42%)
  blocking collectives  11.1 us (19%)
  Pallas kernels  10.4 us (17%)
  waiting for transfers between devices  8.28 us (14%)
  local copies, waits for them, and re-layouts  4.12 us (7%)
    ppermute x11, starting transfers between devices, swapped(): return lax.ppermute(rows_, 'dev', [(i, i ^ bit) for i in range(peers)])  12.9 us
    all_to_all x1, blocking collectives, shards(): lax.all_to_all(outgoing, 'dev', split_axis=0, concat_axis=0, tiled=True)  11.1 us
    ppermute x2, waiting for transfers between devices, passed(): return lax.ppermute(rows_, 'dev', pairs)  7.89 us
    ppermute x2, starting transfers between devices, passed(): return lax.ppermute(rows_, 'dev', pairs)  7.09 us
    pallas_call x4, Pallas kernels, masses_call(): call(kernel, jax.ShapeDtypeStruct(layout or (len(SUMS), n), jnp.float32),...  6.3 us
    all_to_all x1, starting transfers between devices, shards(): lax.all_to_all(facts, 'dev', split_axis=0, concat_axis=0, tiled=True)  5.02 us
    unnamed x9, local copies, waits for them, and re-layouts  3.18 us
    pallas_call x1, Pallas kernels, shards(): call(weights_kernel, jax.ShapeDtypeStruct((1, n), f32))(rank, returned)  1.22 us
  transfers between devices with their start and end apart: 14, of which 4 were waited for; matrix products, arithmetic and copies ran while one was open for 2% of the time, Pallas kernels for 12%

profile of v3, /device:TPU:0, one launch (start us, length us, event | category | flops | bytes accessed | tf_op | source)
XLA Modules:
  0.0 59.5 jit_solution(16989968484469185133)
XLA Ops:
  0.0 0.0 copy-start
  0.0 1.1 %copy-done = bf16[512,768]{1,0:T(8,128)(2,1)S(1)} copy-done((bf16[512,768]{1,0:T(8,128)(2,1)S(1)}, bf16[512,768]{1,0:T(8,128)(2,1)}, u32[]{:S(2)}) %copy-start) | copy-done | bytes 786456
  1.1 0.0 copy-start.1
  1.1 0.7 %copy-done.1 = s32[512]{0:T(512)S(1)} copy-done((s32[512]{0:T(512)S(1)}, s32[512]{0:T(512)}, u32[]{:S(2)}) %copy-start.1) | copy-done | bytes 2072
  1.8 1.0 %shard_map.37 = (bf16[64,768]{1,0:T(8,128)(2,1)S(1)}, bf16[64,768]{1,0:T(8,128)(2,1)S(1)}, bf16[128,768]{1,0:T(8,128)(2,1)S(1)}, bf16[64,768]{1,0:T(8,128)(2,1)S...) custom-call(s32[1,512]{1,0:T(1,128)S(1)} %bitcast.27, ...), custom_call_target="tpu_custom_call" | custom-call | tf_op jit(solution)/shard_map/pallas_call | solution.py:290
  2.9 3.1 %collective-permute-start = (bf16[128,768]{1,0:T(8,128)(2,1)S(1)}, bf16[128,768]{1,0:T(8,128)(2,1)S(1)}, u32[]{:S(2)}, u32[]{:S(2)}) collective-permute-start(bf16[128,768]{1,0:T(8,128)(2,1)S(1)} %get-tuple-element.19.refs_2_), channel_id=1, source_target_pairs={{0,4},{1,5},{2,6},{3,7},{4,0},{5,1},{6,2},{7,3},{8,12},{9,13},{10,... | collective-permute-start | bytes 589832 | tf_op jit(solution)/shard_map/ppermute | solution.py:276
  5.9 2.6 %collective-permute-start.1 = (bf16[64,768]{1,0:T(8,128)(2,1)S(1)}, bf16[64,768]{1,0:T(8,128)(2,1)S(1)}, u32[]{:S(2)}, u32[]{:S(2)}) collective-permute-start(bf16[64,768]{1,0:T(8,128)(2,1)S(1)} %get-tuple-element.20.refs_3_), channel_id=1, source_target_pairs={{0,8},{1,9},{2,10},{3,11},{4,12},{5,13},{6,14},{7,15},{8,0},{9,1},... | collective-permute-start | bytes 294920 | tf_op jit(solution)/shard_map/ppermute | solution.py:276
  8.5 0.0 collective-permute-start.2
  8.5 1.9 %collective-permute-start.3 = (bf16[64,768]{1,0:T(8,128)(2,1)S(1)}, bf16[64,768]{1,0:T(8,128)(2,1)S(1)}, u32[]{:S(2)}, u32[]{:S(2)}) collective-permute-start(bf16[64,768]{1,0:T(8,128)(2,1)S(1)} %get-tuple-element.23.refs_4_), channel_id=1, source_target_pairs={{0,8},{1,9},{2,10},{3,11},{4,12},{5,13},{6,14},{7,15},{8,0},{9,1},... | collective-permute-start | bytes 294920 | tf_op jit(solution)/shard_map/ppermute | solution.py:276
  10.4 1.9 %collective-permute-start.4 = (bf16[64,768]{1,0:T(8,128)(2,1)S(1)}, bf16[64,768]{1,0:T(8,128)(2,1)S(1)}, u32[]{:S(2)}, u32[]{:S(2)}) collective-permute-start(bf16[64,768]{1,0:T(8,128)(2,1)S(1)} %get-tuple-element.24.refs_6_), channel_id=1, source_target_pairs={{0,12},{1,13},{2,14},{3,15},{4,8},{5,9},{6,10},{7,11},{8,4},{9,5},... | collective-permute-start | bytes 294920 | tf_op jit(solution)/shard_map/ppermute | solution.py:276
  12.4 0.0 copy-start.2
  12.4 0.7 %copy-done.2 = s32[512]{0:T(512)S(1)} copy-done((s32[512]{0:T(512)S(1)}, s32[512]{0:T(512)}, u32[]{:S(2)}) %copy-start.2) | copy-done | bytes 2072
  13.0 0.0 copy-start.3
  13.0 0.7 %copy-done.3 = s32[512]{0:T(512)S(1)} copy-done((s32[512]{0:T(512)S(1)}, s32[512]{0:T(512)}, u32[]{:S(2)}) %copy-start.3) | copy-done | bytes 2072
  13.7 1.2 %shard_map.38 = f32[16,8,128]{2,1,0:T(8,128)} custom-call(s32[1,512]{1,0:T(1,128)S(1)} %bitcast.28, s32[1,512]{1,0:T(1,128)S(1)} %bitcast.29, s32[1,512]{1,0:T(1,128)S(1)} %get-tuple-element.17.rank_ref, bf16[64,768]{1,0:T(8,128)(2,1)S(1)} %get-tuple-element.18.refs_0_, bf16[64,768]{1,0:T(8,128)(2,1)S(1)} %get-tuple-element.22.refs_1_, ...), custom_call_target="tpu_custom_call" | custom-call | tf_op jit(solution)/shard_map/pallas_call | solution.py:321
  14.9 0.0 collective-permute-done
  14.9 5.0 %all-to-all-start = ((f32[16,8,128]{2,1,0:T(8,128)}), f32[16,8,128]{2,1,0:T(8,128)S(1)}, u32[]{:S(2)}, u32[]{:S(2)}) async-start(f32[16,8,128]{2,1,0:T(8,128)} %shard_map.38), calls=%async_computation | async-start | bytes 131072 | tf_op jit(solution)/shard_map/all_to_all | solution.py:338
  20.0 0.0 collective-permute-done.1
  20.0 0.0 collective-permute-done.2
  20.0 0.5 collective-permute-start.5
  20.5 1.7 %collective-permute-start.6 = (bf16[256,768]{1,0:T(8,128)(2,1)S(1)}, bf16[256,768]{1,0:T(8,128)(2,1)S(1)}, u32[]{:S(2)}, u32[]{:S(2)}) collective-permute-start(bf16[256,768]{1,0:T(8,128)(2,1)S(1)} %pad_maximum_fusion.refs_0_), channel_id=1, source_target_pairs={{0,2},{1,3},{2,0},{3,1},{4,6},{5,7},{6,4},{7,5},{8,10},{9,11},{10,... | collective-permute-start | bytes 1179656 | tf_op jit(solution)/shard_map/ppermute | solution.py:276
  22.2 5.8 %collective-permute-start.8 = (bf16[256,768]{1,0:T(8,128)(2,1)S(1)}, bf16[256,768]{1,0:T(8,128)(2,1)}, u32[]{:S(2)}, u32[]{:S(2)}) collective-permute-start(bf16[256,768]{1,0:T(8,128)(2,1)S(1)} %pad_maximum_fusion.refs_0_), channel_id=1, source_target_pairs={{0,4},{1,5},{2,6},{3,7},{4,8},{5,9},{6,10},{7,11},{8,12},{9,13},{1... | collective-permute-start | bytes 1179656 | tf_op jit(solution)/shard_map/ppermute | solution.py:280
  28.0 0.0 collective-permute-done.3
  28.0 0.0 collective-permute-done.4
  28.0 0.2 all-to-all-done
  28.3 0.1 reshape_reshape.15
  28.6 0.1 reshape.133
  28.7 0.1 rev.32
  28.9 0.1 reshape.132
  29.0 0.6 %shard_map.39 = f32[1,2560]{1,0:T(1,128)S(1)} custom-call(s32[1,2560]{1,0:T(1,128)S(1)} %fusion.2.place_ref, f32[48,128]{1,0:T(8,128)S(1)} %fusion.1.table_ref), custom_call_target="tpu_custom_call" | custom-call | tf_op jit(solution)/shard_map/pallas_call | solution.py:369
  29.7 0.0 collective-permute-done.5.refs_2_
  29.7 0.1 collective-permute-start.11
  29.8 1.3 %collective-permute-start.9 = (bf16[256,768]{1,0:T(8,128)(2,1)S(1)}, bf16[256,768]{1,0:T(8,128)(2,1)}, u32[]{:S(2)}, u32[]{:S(2)}) collective-permute-start(bf16[256,768]{1,0:T(8,128)(2,1)S(1)} %pad_maximum_fusion.1.refs_1_), channel_id=1, source_target_pairs={{4,0},{5,1},{6,2},{7,3},{8,4},{9,5},{10,6},{11,7},{12,8},{13,9},{1... | collective-permute-start | bytes 1179656 | tf_op jit(solution)/shard_map/ppermute | solution.py:280
  31.1 0.4 copy.16.refs_6_.refs_5_.refs_8_.refs_7_
  31.6 0.7 %collective-permute-start.7 = (bf16[256,768]{1,0:T(8,128)(2,1)S(1)}, bf16[256,768]{1,0:T(8,128)(2,1)S(1)}, u32[]{:S(2)}, u32[]{:S(2)}) collective-permute-start(bf16[256,768]{1,0:T(8,128)(2,1)S(1)} %pad_maximum_fusion.1.refs_1_), channel_id=1, source_target_pairs={{0,2},{1,3},{2,0},{3,1},{4,6},{5,7},{6,4},{7,5},{8,10},{9,11},{10,... | collective-permute-start | bytes 1179656 | tf_op jit(solution)/shard_map/ppermute | solution.py:276
  32.3 0.1 collective-permute-done.6.refs_4_.refs_2_
  32.4 0.0 collective-permute-done.11.refs_3_
  32.4 1.4 %shard_map.40.refs_6_ = f32[8,256]{1,0:T(8,128)S(1)} custom-call(bf16[256,768]{1,0:T(8,128)(2,1)S(1)} %pad_maximum_fusion.refs_0_, bf16[256,768]{1,0:T(8,128)(2,1)S(1)} %pad_maximum_fusion.1.refs_1_, bf16[256,768]{1,0:T(8,128)(2,1)S(1)} %collective-permute-done.5.refs_2_, bf16[256,768]{1,0:T(8,128)(2,1)S(1)} %collective-permute-done.11.refs_3_, ...), custom_call_target="tpu_custom_call" | custom-call | tf_op jit(solution)/shard_map/pallas_call | solution.py:222
  33.8 2.1 %collective-permute-done.8.refs_3_.refs_5_ = bf16[256,768]{1,0:T(8,128)(2,1)} collective-permute-done((bf16[256,768]{1,0:T(8,128)(2,1)S(1)}, bf16[256,768]{1,0:T(8,128)(2,1)}, u32[]{:S(2)}, u32[]{:S(2)}) %collective-permute-start.8) | collective-permute-done | bytes 393248 | tf_op jit(solution)/shard_map/ppermute | solution.py:280
  35.9 1.6 %shard_map.41.refs_9_ = f32[8,256]{1,0:T(8,128)S(1)} custom-call(bf16[256,768]{1,0:T(8,128)(2,1)S(1)} %pad_maximum_fusion.refs_0_, bf16[256,768]{1,0:T(8,128)(2,1)S(1)} %pad_maximum_fusion.1.refs_1_, bf16[256,768]{1,0:T(8,128)(2,1)S(1)} %collective-permute-done.6.refs_4_.refs_2_, bf16[256,768]{1,0:T(8,128)(2,1)} %collective-permute-done.8.refs_3_.refs_5_, ...), custom_call_target="tpu_custom_call" | custom-call | tf_op jit(solution)/shard_map/pallas_call | solution.py:222
  37.5 5.8 %collective-permute-done.9.refs_6_ = bf16[256,768]{1,0:T(8,128)(2,1)} collective-permute-done((bf16[256,768]{1,0:T(8,128)(2,1)S(1)}, bf16[256,768]{1,0:T(8,128)(2,1)}, u32[]{:S(2)}, u32[]{:S(2)}) %collective-permute-start.9) | collective-permute-done | bytes 393248 | tf_op jit(solution)/shard_map/ppermute | solution.py:280
  43.3 0.0 collective-permute-start.12
  43.3 0.5 collective-permute-start.10
  43.8 0.0 collective-permute-done.7.refs_4_.refs_3_
  43.8 2.2 %shard_map.42.refs_8_ = f32[8,256]{1,0:T(8,128)S(1)} custom-call(bf16[256,768]{1,0:T(8,128)(2,1)S(1)} %pad_maximum_fusion.refs_0_, bf16[256,768]{1,0:T(8,128)(2,1)S(1)} %pad_maximum_fusion.1.refs_1_, bf16[256,768]{1,0:T(8,128)(2,1)S(1)} %collective-permute-done.5.refs_2_, bf16[256,768]{1,0:T(8,128)(2,1)S(1)} %collective-permute-done.11.refs_3_, ...), custom_call_target="tpu_custom_call" | custom-call | tf_op jit(solution)/shard_map/pallas_call | solution.py:222
  46.0 0.0 collective-permute-done.12.refs_5_
  46.0 0.0 collective-permute-done.10.refs_4_
  46.0 1.1 %shard_map.43 = f32[16,2,128]{2,1,0:T(2,128)S(1)} custom-call(bf16[256,768]{1,0:T(8,128)(2,1)S(1)} %pad_maximum_fusion.refs_0_, bf16[256,768]{1,0:T(8,128)(2,1)S(1)} %pad_maximum_fusion.1.refs_1_, bf16[256,768]{1,0:T(8,128)(2,1)S(1)} %collective-permute-done.6.refs_4_.refs_2_, bf16[256,768]{1,0:T(8,128)(2,1)S(1)} %collective-permute-done.7.refs_4_.refs_3_, ...), custom_call_target="tpu_custom_call" | custom-call | tf_op jit(solution)/shard_map/pallas_call | solution.py:222
  47.1 11.1 %all_to_all.10.returned_ref = f32[16,2,128]{2,1,0:T(2,128)S(1)} all-to-all(f32[16,2,128]{2,1,0:T(2,128)S(1)} %shard_map.43), channel_id=1, replica_groups=mesh['grp'=2,'dev'=16] {'dev'}, dimensions={0} | all-to-all | bytes 32768 | tf_op jit(solution)/shard_map/all_to_all | solution.py:415
  58.3 1.2 %shard_map.44 = f32[1,512]{1,0:T(1,128)} custom-call(s32[1,512]{1,0:T(1,128)S(1)} %get-tuple-element.17.rank_ref, f32[16,2,128]{2,1,0:T(2,128)S(1)} %all_to_all.10.returned_ref), custom_call_target="tpu_custom_call" | custom-call | tf_op jit(solution)/shard_map/pallas_call | solution.py:416
  (31 shorter events, 0.4 us)
Async XLA Ops:
  0.0 1.1 %copy-start = (bf16[512,768]{1,0:T(8,128)(2,1)S(1)}, bf16[512,768]{1,0:T(8,128)(2,1)}, u32[]{:S(2)}) copy-start(bf16[512,768]{1,0:T(8,128)(2,1)} %rows_hbm.1) | copy-start | bytes 2359300
  1.1 0.7 %copy-start.1 = (s32[512]{0:T(512)S(1)}, s32[512]{0:T(512)}, u32[]{:S(2)}) copy-start(s32[512]{0:T(512)} %param.4) | copy-start | bytes 6148
  2.9 12.0 %collective-permute-start = (bf16[128,768]{1,0:T(8,128)(2,1)S(1)}, bf16[128,768]{1,0:T(8,128)(2,1)S(1)}, u32[]{:S(2)}, u32[]{:S(2)}) collective-permute-start(bf16[128,768]{1,0:T(8,128)(2,1)S(1)} %get-tuple-element.19.refs_2_), channel_id=1, source_target_pairs={{0,4},{1,5},{2,6},{3,7},{4,0},{5,1},{6,2},{7,3},{8,12},{9,13},{10,... | collective-permute-start | bytes 589832 | tf_op jit(solution)/shard_map/ppermute | solution.py:276
  5.9 14.0 %collective-permute-start.1 = (bf16[64,768]{1,0:T(8,128)(2,1)S(1)}, bf16[64,768]{1,0:T(8,128)(2,1)S(1)}, u32[]{:S(2)}, u32[]{:S(2)}) collective-permute-start(bf16[64,768]{1,0:T(8,128)(2,1)S(1)} %get-tuple-element.20.refs_3_), channel_id=1, source_target_pairs={{0,8},{1,9},{2,10},{3,11},{4,12},{5,13},{6,14},{7,15},{8,0},{9,1},... | collective-permute-start | bytes 294920 | tf_op jit(solution)/shard_map/ppermute | solution.py:276
  8.5 11.4 %collective-permute-start.2 = (bf16[64,768]{1,0:T(8,128)(2,1)S(1)}, bf16[64,768]{1,0:T(8,128)(2,1)S(1)}, u32[]{:S(2)}, u32[]{:S(2)}) collective-permute-start(bf16[64,768]{1,0:T(8,128)(2,1)S(1)} %get-tuple-element.21.refs_5_), channel_id=1, source_target_pairs={{0,12},{1,13},{2,14},{3,15},{4,8},{5,9},{6,10},{7,11},{8,4},{9,5},... | collective-permute-start | bytes 294920 | tf_op jit(solution)/shard_map/ppermute | solution.py:276
  8.5 19.4 %collective-permute-start.3 = (bf16[64,768]{1,0:T(8,128)(2,1)S(1)}, bf16[64,768]{1,0:T(8,128)(2,1)S(1)}, u32[]{:S(2)}, u32[]{:S(2)}) collective-permute-start(bf16[64,768]{1,0:T(8,128)(2,1)S(1)} %get-tuple-element.23.refs_4_), channel_id=1, source_target_pairs={{0,8},{1,9},{2,10},{3,11},{4,12},{5,13},{6,14},{7,15},{8,0},{9,1},... | collective-permute-start | bytes 294920 | tf_op jit(solution)/shard_map/ppermute | solution.py:276
  10.4 17.5 %collective-permute-start.4 = (bf16[64,768]{1,0:T(8,128)(2,1)S(1)}, bf16[64,768]{1,0:T(8,128)(2,1)S(1)}, u32[]{:S(2)}, u32[]{:S(2)}) collective-permute-start(bf16[64,768]{1,0:T(8,128)(2,1)S(1)} %get-tuple-element.24.refs_6_), channel_id=1, source_target_pairs={{0,12},{1,13},{2,14},{3,15},{4,8},{5,9},{6,10},{7,11},{8,4},{9,5},... | collective-permute-start | bytes 294920 | tf_op jit(solution)/shard_map/ppermute | solution.py:276
  12.4 0.7 %copy-start.2 = (s32[512]{0:T(512)S(1)}, s32[512]{0:T(512)}, u32[]{:S(2)}) copy-start(s32[512]{0:T(512)} %param.4) | copy-start | bytes 6148
  13.0 0.7 %copy-start.3 = (s32[512]{0:T(512)S(1)}, s32[512]{0:T(512)}, u32[]{:S(2)}) copy-start(s32[512]{0:T(512)} %param.5) | copy-start | bytes 6148
  14.9 13.3 %all-to-all-start = ((f32[16,8,128]{2,1,0:T(8,128)}), f32[16,8,128]{2,1,0:T(8,128)S(1)}, u32[]{:S(2)}, u32[]{:S(2)}) async-start(f32[16,8,128]{2,1,0:T(8,128)} %shard_map.38), calls=%async_computation | async-start | bytes 131072 | tf_op jit(solution)/shard_map/all_to_all | solution.py:338
  20.0 9.7 %collective-permute-start.5 = (bf16[256,768]{1,0:T(8,128)(2,1)S(1)}, bf16[256,768]{1,0:T(8,128)(2,1)S(1)}, u32[]{:S(2)}, u32[]{:S(2)}) collective-permute-start(bf16[256,768]{1,0:T(8,128)(2,1)S(1)} %pad_maximum_fusion.refs_0_), channel_id=1, source_target_pairs={{0,1},{1,0},{2,3},{3,2},{4,5},{5,4},{6,7},{7,6},{8,9},{9,8},{10,11... | collective-permute-start | bytes 1179656 | tf_op jit(solution)/shard_map/ppermute | solution.py:276
  20.5 11.9 %collective-permute-start.6 = (bf16[256,768]{1,0:T(8,128)(2,1)S(1)}, bf16[256,768]{1,0:T(8,128)(2,1)S(1)}, u32[]{:S(2)}, u32[]{:S(2)}) collective-permute-start(bf16[256,768]{1,0:T(8,128)(2,1)S(1)} %pad_maximum_fusion.refs_0_), channel_id=1, source_target_pairs={{0,2},{1,3},{2,0},{3,1},{4,6},{5,7},{6,4},{7,5},{8,10},{9,11},{10,... | collective-permute-start | bytes 1179656 | tf_op jit(solution)/shard_map/ppermute | solution.py:276
  22.2 13.7 %collective-permute-start.8 = (bf16[256,768]{1,0:T(8,128)(2,1)S(1)}, bf16[256,768]{1,0:T(8,128)(2,1)}, u32[]{:S(2)}, u32[]{:S(2)}) collective-permute-start(bf16[256,768]{1,0:T(8,128)(2,1)S(1)} %pad_maximum_fusion.refs_0_), channel_id=1, source_target_pairs={{0,4},{1,5},{2,6},{3,7},{4,8},{5,9},{6,10},{7,11},{8,12},{9,13},{1... | collective-permute-start | bytes 1179656 | tf_op jit(solution)/shard_map/ppermute | solution.py:280
  29.7 2.7 %collective-permute-start.11 = (bf16[256,768]{1,0:T(8,128)(2,1)S(1)}, bf16[256,768]{1,0:T(8,128)(2,1)S(1)}, u32[]{:S(2)}, u32[]{:S(2)}) collective-permute-start(bf16[256,768]{1,0:T(8,128)(2,1)S(1)} %pad_maximum_fusion.1.refs_1_), channel_id=1, source_target_pairs={{0,1},{1,0},{2,3},{3,2},{4,5},{5,4},{6,7},{7,6},{8,9},{9,8},{10,11... | collective-permute-start | bytes 1179656 | tf_op jit(solution)/shard_map/ppermute | solution.py:276
  29.8 13.5 %collective-permute-start.9 = (bf16[256,768]{1,0:T(8,128)(2,1)S(1)}, bf16[256,768]{1,0:T(8,128)(2,1)}, u32[]{:S(2)}, u32[]{:S(2)}) collective-permute-start(bf16[256,768]{1,0:T(8,128)(2,1)S(1)} %pad_maximum_fusion.1.refs_1_), channel_id=1, source_target_pairs={{4,0},{5,1},{6,2},{7,3},{8,4},{9,5},{10,6},{11,7},{12,8},{13,9},{1... | collective-permute-start | bytes 1179656 | tf_op jit(solution)/shard_map/ppermute | solution.py:280
  31.6 12.2 %collective-permute-start.7 = (bf16[256,768]{1,0:T(8,128)(2,1)S(1)}, bf16[256,768]{1,0:T(8,128)(2,1)S(1)}, u32[]{:S(2)}, u32[]{:S(2)}) collective-permute-start(bf16[256,768]{1,0:T(8,128)(2,1)S(1)} %pad_maximum_fusion.1.refs_1_), channel_id=1, source_target_pairs={{0,2},{1,3},{2,0},{3,1},{4,6},{5,7},{6,4},{7,5},{8,10},{9,11},{10,... | collective-permute-start | bytes 1179656 | tf_op jit(solution)/shard_map/ppermute | solution.py:276
  43.3 2.7 %collective-permute-start.12 = (bf16[256,768]{1,0:T(8,128)(2,1)}, bf16[256,768]{1,0:T(8,128)(2,1)S(1)}, u32[]{:S(2)}, u32[]{:S(2)}) collective-permute-start(bf16[256,768]{1,0:T(8,128)(2,1)} %collective-permute-done.9.refs_6_), channel_id=1, source_target_pairs={{0,1},{1,0},{2,3},{3,2},{4,5},{5,4},{6,7},{7,6},{8,9},{9,8},{10,11... | collective-permute-start | bytes 1179656 | tf_op jit(solution)/shard_map/ppermute | solution.py:276
  43.3 2.7 %collective-permute-start.10 = (bf16[256,768]{1,0:T(8,128)(2,1)}, bf16[256,768]{1,0:T(8,128)(2,1)S(1)}, u32[]{:S(2)}, u32[]{:S(2)}) collective-permute-start(bf16[256,768]{1,0:T(8,128)(2,1)} %collective-permute-done.8.refs_3_.refs_5_), channel_id=1, source_target_pairs={{0,1},{1,0},{2,3},{3,2},{4,5},{5,4},{6,7},{7,6},{8,9},{9,8},{10,11... | collective-permute-start | bytes 1179656 | tf_op jit(solution)/shard_map/ppermute | solution.py:276

commit v4 on v1

--- a/solution.py
+++ b/solution.py
@@ -13,7 +13,7 @@
 SIMILARITY_CUTOFF = 0.9
 SOFTMAX_HEAT = 0.02
 SCALE = math.log2(math.e) / SOFTMAX_HEAT
-SHIFT = SIMILARITY_CUTOFF * SCALE
+FACTOR = math.exp(-SIMILARITY_CUTOFF / SOFTMAX_HEAT)
 QUAD = 4
 CHUNK = 256
 LANES = 128
@@ -148,7 +148,7 @@
         at, to = NAMES.index(down) * n, NAMES.index(across) * n
         scale = self.columns[at : at + n, 0:1]
         label = self.columns[at : at + n, 1:2]
-        power = products * scale * self.rows[0:1, to : to + n] - SHIFT
+        power = products * scale * self.rows[0:1, to : to + n]
         mask = label == self.rows[1:2, to : to + n]
         if down == across:
             mask &= iota((n, n), 0) != iota((n, n), 1)
@@ -251,7 +251,7 @@
 
     mass = chosen(0, slab, jnp.where(upper, m + member, member))
     mass += chosen(1, jnp.where(upper, slab + 1, slab - 1), jnp.where(upper, member, m + member))
-    out_ref[...] = 1.0 / (1.0 + mass)
+    out_ref[...] = 1.0 / (1.0 + mass * FACTOR)
 
 
 def xor_order(array, axis, bits):
@@ -390,14 +390,15 @@
         + [("b0l", "b0l"), ("b0h", "b0l"), ("b1h", "b0l"), ("b2h", "b0l")]
         + [("b1l", "b0h"), ("b1l", "b0l"), ("b1l", "b2h")]
     )
-    arrays["u1"] = swapped(after_all(arrays['u'], arrays["b2h"]), 1)
-    masses = masses_after([(u, b) for u in ("u", "u1") for b in ("b0h", "b0l", "b2h")], masses)
-    arrays["l1"] = swapped(after_all(arrays["l"], masses, arrays["b2l"]), 1)
+    masses = masses_after([("u", "b0h"), ("u", "b0l"), ("u", "b2h")], masses)
+    arrays["u1"] = swapped(after_all(arrays["u"], arrays["l"]), 1)
+    arrays["l1"] = swapped(after_all(arrays["l"], masses), 1)
     masses = masses_after(
-        [("b2l", "b0h"), ("b2l", "b0l"), ("b1h", "b2l"), ("b1l", "b2l"), ("u", "b2l"), ("u1", "b2l")],
+        [("b2l", "b0h"), ("b2l", "b0l"), ("b1h", "b2l"), ("b1l", "b2l")]
+        + [("u", "b2l"), ("l", "b0l"), ("l", "b2l")],
         masses,
     )
-    last = [("l", "b0l"), ("l", "b2l"), ("l1", "b0l"), ("l1", "b2l")]
+    last = [("u1", b) for b in ("b0h", "b0l", "b2h", "b2l")] + [("l1", "b0l"), ("l1", "b2l")]
     if by_permutes:
         outgoing = masses_call(last, arrays, rows, columns, masses, (peers, 2, 2 * per_half))
     else:

time: 59.9 us -> 59.9 us (level)
  Pallas kernels: 12.7 us -> 10.3 us
  starting transfers between devices: 24.4 us -> 25.7 us
  blocking collectives: 10.4 us -> 11.2 us
    pallas_call x4, Pallas kernels: 8.6 us -> 6.24 us  [masses_call(): call(kernel, jax.ShapeDtypeStruct(layout or (len(SUMS), n), jnp.float32),...]
    ppermute x2, waiting for transfers between devices: 5.65 us -> 7.91 us  [passed(): return lax.ppermute(rows_, 'dev', pairs)]
    ppermute x11, waiting for transfers between devices: 1.33 us -> 0.14 us  [swapped(): return lax.ppermute(rows_, 'dev', [(i, i ^ bit) for i in range(peers)])]
    ppermute x2, starting transfers between devices: 6.34 us -> 7.09 us  [passed(): return lax.ppermute(rows_, 'dev', pairs)]
    all_to_all x1, blocking collectives: 10.4 us -> 11.2 us  [shards(): lax.all_to_all(outgoing, 'dev', split_axis=0, concat_axis=0, tiled=True)]
    all_to_all x1, waiting for transfers between devices: 0.96 us -> 0.25 us  [shards(): lax.all_to_all(facts, 'dev', split_axis=0, concat_axis=0, tiled=True)]
  transfers between devices with their start and end apart: 14 -> 14, of which waited for: 5 -> 4; matrix products, arithmetic and copies ran while one was open for 2% -> 2% of each run, Pallas kernels for 14% -> 12%
where the time goes in v4:
time: 59.9 us; the launch traced here: 59.5 us
  starting transfers between devices  25.7 us (43%)
  blocking collectives  11.2 us (19%)
  Pallas kernels  10.3 us (17%)
  waiting for transfers between devices  8.31 us (14%)
  local copies, waits for them, and re-layouts  3.44 us (6%)
    ppermute x11, starting transfers between devices, swapped(): return lax.ppermute(rows_, 'dev', [(i, i ^ bit) for i in range(peers)])  12.9 us
    all_to_all x1, blocking collectives, shards(): lax.all_to_all(outgoing, 'dev', split_axis=0, concat_axis=0, tiled=True)  11.2 us
    ppermute x2, waiting for transfers between devices, passed(): return lax.ppermute(rows_, 'dev', pairs)  7.91 us
    ppermute x2, starting transfers between devices, passed(): return lax.ppermute(rows_, 'dev', pairs)  7.09 us
    pallas_call x4, Pallas kernels, masses_call(): call(kernel, jax.ShapeDtypeStruct(layout or (len(SUMS), n), jnp.float32),...  6.24 us
    all_to_all x1, starting transfers between devices, shards(): lax.all_to_all(facts, 'dev', split_axis=0, concat_axis=0, tiled=True)  5.69 us
    unnamed x7, local copies, waits for them, and re-layouts  2.5 us
    pallas_call x1, Pallas kernels, shards(): call(weights_kernel, jax.ShapeDtypeStruct((1, n), f32))(rank, returned)  1.22 us
  transfers between devices with their start and end apart: 14, of which 4 were waited for; matrix products, arithmetic and copies ran while one was open for 2% of the time, Pallas kernels for 12%

profile of v4, /device:TPU:0, one launch (start us, length us, event | category | flops | bytes accessed | tf_op | source)
XLA Modules:
  0.0 59.5 jit_solution(9417890181026676406)
XLA Ops:
  0.0 0.0 copy-start
  0.0 1.1 %copy-done = bf16[512,768]{1,0:T(8,128)(2,1)S(1)} copy-done((bf16[512,768]{1,0:T(8,128)(2,1)S(1)}, bf16[512,768]{1,0:T(8,128)(2,1)}, u32[]{:S(2)}) %copy-start) | copy-done | bytes 786456
  1.1 0.0 copy-start.1
  1.1 0.7 %copy-done.1 = s32[512]{0:T(512)S(1)} copy-done((s32[512]{0:T(512)S(1)}, s32[512]{0:T(512)}, u32[]{:S(2)}) %copy-start.1) | copy-done | bytes 2072
  1.8 1.0 %shard_map.37 = (bf16[64,768]{1,0:T(8,128)(2,1)S(1)}, bf16[64,768]{1,0:T(8,128)(2,1)S(1)}, bf16[128,768]{1,0:T(8,128)(2,1)S(1)}, bf16[64,768]{1,0:T(8,128)(2,1)S...) custom-call(s32[1,512]{1,0:T(1,128)S(1)} %bitcast.27, ...), custom_call_target="tpu_custom_call" | custom-call | tf_op jit(solution)/shard_map/pallas_call | solution.py:294
  2.9 3.1 %collective-permute-start = (bf16[128,768]{1,0:T(8,128)(2,1)S(1)}, bf16[128,768]{1,0:T(8,128)(2,1)S(1)}, u32[]{:S(2)}, u32[]{:S(2)}) collective-permute-start(bf16[128,768]{1,0:T(8,128)(2,1)S(1)} %get-tuple-element.19.refs_2_), channel_id=1, source_target_pairs={{0,4},{1,5},{2,6},{3,7},{4,0},{5,1},{6,2},{7,3},{8,12},{9,13},{10,... | collective-permute-start | bytes 589832 | tf_op jit(solution)/shard_map/ppermute | solution.py:280
  5.9 2.6 %collective-permute-start.1 = (bf16[64,768]{1,0:T(8,128)(2,1)S(1)}, bf16[64,768]{1,0:T(8,128)(2,1)S(1)}, u32[]{:S(2)}, u32[]{:S(2)}) collective-permute-start(bf16[64,768]{1,0:T(8,128)(2,1)S(1)} %get-tuple-element.20.refs_3_), channel_id=1, source_target_pairs={{0,8},{1,9},{2,10},{3,11},{4,12},{5,13},{6,14},{7,15},{8,0},{9,1},... | collective-permute-start | bytes 294920 | tf_op jit(solution)/shard_map/ppermute | solution.py:280
  8.5 0.0 collective-permute-start.2
  8.5 1.9 %collective-permute-start.3 = (bf16[64,768]{1,0:T(8,128)(2,1)S(1)}, bf16[64,768]{1,0:T(8,128)(2,1)S(1)}, u32[]{:S(2)}, u32[]{:S(2)}) collective-permute-start(bf16[64,768]{1,0:T(8,128)(2,1)S(1)} %get-tuple-element.23.refs_4_), channel_id=1, source_target_pairs={{0,8},{1,9},{2,10},{3,11},{4,12},{5,13},{6,14},{7,15},{8,0},{9,1},... | collective-permute-start | bytes 294920 | tf_op jit(solution)/shard_map/ppermute | solution.py:280
  10.4 1.9 %collective-permute-start.4 = (bf16[64,768]{1,0:T(8,128)(2,1)S(1)}, bf16[64,768]{1,0:T(8,128)(2,1)S(1)}, u32[]{:S(2)}, u32[]{:S(2)}) collective-permute-start(bf16[64,768]{1,0:T(8,128)(2,1)S(1)} %get-tuple-element.24.refs_6_), channel_id=1, source_target_pairs={{0,12},{1,13},{2,14},{3,15},{4,8},{5,9},{6,10},{7,11},{8,4},{9,5},... | collective-permute-start | bytes 294920 | tf_op jit(solution)/shard_map/ppermute | solution.py:280
  12.4 0.0 copy-start.2
  12.4 0.7 %copy-done.2 = s32[512]{0:T(512)S(1)} copy-done((s32[512]{0:T(512)S(1)}, s32[512]{0:T(512)}, u32[]{:S(2)}) %copy-start.2) | copy-done | bytes 2072
  13.0 1.2 %shard_map.38 = f32[16,8,128]{2,1,0:T(8,128)} custom-call(s32[1,512]{1,0:T(1,128)S(1)} %bitcast.28, s32[2,512]{1,0:T(2,128)S(1)} %get-tuple-element.17.rank_ref, bf16[64,768]{1,0:T(8,128)(2,1)S(1)} %get-tuple-element.18.refs_0_, bf16[64,768]{1,0:T(8,128)(2,1)S(1)} %get-tuple-element.22.refs_1_, bf16[128,768]{1,0:T(8,128)(2,1)S(1)} %get-tuple-element.19.refs_2_, ...), custom_call_target="tpu_custom_call" | custom-call | tf_op jit(solution)/shard_map/pallas_call | solution.py:325
  14.2 0.0 collective-permute-done
  14.2 5.7 %all-to-all-start = ((f32[16,8,128]{2,1,0:T(8,128)}), f32[16,8,128]{2,1,0:T(8,128)S(1)}, u32[]{:S(2)}, u32[]{:S(2)}) async-start(f32[16,8,128]{2,1,0:T(8,128)} %shard_map.38), calls=%async_computation | async-start | bytes 131072 | tf_op jit(solution)/shard_map/all_to_all | solution.py:345
  20.0 0.0 collective-permute-done.1
  20.0 0.0 collective-permute-done.2
  20.0 0.5 collective-permute-start.5
  20.5 1.7 %collective-permute-start.6 = (bf16[256,768]{1,0:T(8,128)(2,1)S(1)}, bf16[256,768]{1,0:T(8,128)(2,1)S(1)}, u32[]{:S(2)}, u32[]{:S(2)}) collective-permute-start(bf16[256,768]{1,0:T(8,128)(2,1)S(1)} %pad_maximum_fusion.refs_0_), channel_id=1, source_target_pairs={{0,2},{1,3},{2,0},{3,1},{4,6},{5,7},{6,4},{7,5},{8,10},{9,11},{10,... | collective-permute-start | bytes 1179656 | tf_op jit(solution)/shard_map/ppermute | solution.py:280
  22.2 5.8 %collective-permute-start.8 = (bf16[256,768]{1,0:T(8,128)(2,1)S(1)}, bf16[256,768]{1,0:T(8,128)(2,1)}, u32[]{:S(2)}, u32[]{:S(2)}) collective-permute-start(bf16[256,768]{1,0:T(8,128)(2,1)S(1)} %pad_maximum_fusion.refs_0_), channel_id=1, source_target_pairs={{0,4},{1,5},{2,6},{3,7},{4,8},{5,9},{6,10},{7,11},{8,12},{9,13},{1... | collective-permute-start | bytes 1179656 | tf_op jit(solution)/shard_map/ppermute | solution.py:284
  28.0 0.0 collective-permute-done.3
  28.0 0.0 collective-permute-done.4
  28.0 0.3 all-to-all-done
  28.3 0.1 reshape_reshape.15
  28.6 0.1 reshape.133
  28.7 0.1 rev.32
  28.9 0.1 reshape.132
  29.0 0.6 %shard_map.39 = f32[1,2560]{1,0:T(1,128)S(1)} custom-call(s32[1,2560]{1,0:T(1,128)S(1)} %fusion.2.place_ref, f32[48,128]{1,0:T(8,128)S(1)} %fusion.1.table_ref), custom_call_target="tpu_custom_call" | custom-call | tf_op jit(solution)/shard_map/pallas_call | solution.py:376
  29.7 0.0 collective-permute-done.5.refs_2_
  29.7 0.1 collective-permute-start.11
  29.8 1.3 %collective-permute-start.9 = (bf16[256,768]{1,0:T(8,128)(2,1)S(1)}, bf16[256,768]{1,0:T(8,128)(2,1)}, u32[]{:S(2)}, u32[]{:S(2)}) collective-permute-start(bf16[256,768]{1,0:T(8,128)(2,1)S(1)} %pad_maximum_fusion.1.refs_1_), channel_id=1, source_target_pairs={{4,0},{5,1},{6,2},{7,3},{8,4},{9,5},{10,6},{11,7},{12,8},{13,9},{1... | collective-permute-start | bytes 1179656 | tf_op jit(solution)/shard_map/ppermute | solution.py:284
  31.1 0.4 copy.16.refs_6_.refs_5_.refs_8_.refs_7_
  31.6 0.7 %collective-permute-start.7 = (bf16[256,768]{1,0:T(8,128)(2,1)S(1)}, bf16[256,768]{1,0:T(8,128)(2,1)S(1)}, u32[]{:S(2)}, u32[]{:S(2)}) collective-permute-start(bf16[256,768]{1,0:T(8,128)(2,1)S(1)} %pad_maximum_fusion.1.refs_1_), channel_id=1, source_target_pairs={{0,2},{1,3},{2,0},{3,1},{4,6},{5,7},{6,4},{7,5},{8,10},{9,11},{10,... | collective-permute-start | bytes 1179656 | tf_op jit(solution)/shard_map/ppermute | solution.py:280
  32.3 0.1 collective-permute-done.6.refs_4_.refs_2_
  32.4 0.0 collective-permute-done.11.refs_3_
  32.4 1.4 %shard_map.40.refs_6_ = f32[8,256]{1,0:T(8,128)S(1)} custom-call(bf16[256,768]{1,0:T(8,128)(2,1)S(1)} %pad_maximum_fusion.refs_0_, bf16[256,768]{1,0:T(8,128)(2,1)S(1)} %pad_maximum_fusion.1.refs_1_, bf16[256,768]{1,0:T(8,128)(2,1)S(1)} %collective-permute-done.5.refs_2_, bf16[256,768]{1,0:T(8,128)(2,1)S(1)} %collective-permute-done.11.refs_3_, ...), custom_call_target="tpu_custom_call" | custom-call | tf_op jit(solution)/shard_map/pallas_call | solution.py:226
  33.8 2.1 %collective-permute-done.8.refs_3_.refs_5_ = bf16[256,768]{1,0:T(8,128)(2,1)} collective-permute-done((bf16[256,768]{1,0:T(8,128)(2,1)S(1)}, bf16[256,768]{1,0:T(8,128)(2,1)}, u32[]{:S(2)}, u32[]{:S(2)}) %collective-permute-start.8) | collective-permute-done | bytes 393248 | tf_op jit(solution)/shard_map/ppermute | solution.py:284
  35.9 1.6 %shard_map.41.refs_9_ = f32[8,256]{1,0:T(8,128)S(1)} custom-call(bf16[256,768]{1,0:T(8,128)(2,1)S(1)} %pad_maximum_fusion.refs_0_, bf16[256,768]{1,0:T(8,128)(2,1)S(1)} %pad_maximum_fusion.1.refs_1_, bf16[256,768]{1,0:T(8,128)(2,1)S(1)} %collective-permute-done.6.refs_4_.refs_2_, bf16[256,768]{1,0:T(8,128)(2,1)} %collective-permute-done.8.refs_3_.refs_5_, ...), custom_call_target="tpu_custom_call" | custom-call | tf_op jit(solution)/shard_map/pallas_call | solution.py:226
  37.5 5.8 %collective-permute-done.9.refs_6_ = bf16[256,768]{1,0:T(8,128)(2,1)} collective-permute-done((bf16[256,768]{1,0:T(8,128)(2,1)S(1)}, bf16[256,768]{1,0:T(8,128)(2,1)}, u32[]{:S(2)}, u32[]{:S(2)}) %collective-permute-start.9) | collective-permute-done | bytes 393248 | tf_op jit(solution)/shard_map/ppermute | solution.py:284
  43.3 0.0 collective-permute-start.12
  43.3 0.5 collective-permute-start.10
  43.8 0.0 collective-permute-done.7.refs_4_.refs_3_
  43.8 2.2 %shard_map.42.refs_8_ = f32[8,256]{1,0:T(8,128)S(1)} custom-call(bf16[256,768]{1,0:T(8,128)(2,1)S(1)} %pad_maximum_fusion.refs_0_, bf16[256,768]{1,0:T(8,128)(2,1)S(1)} %pad_maximum_fusion.1.refs_1_, bf16[256,768]{1,0:T(8,128)(2,1)S(1)} %collective-permute-done.5.refs_2_, bf16[256,768]{1,0:T(8,128)(2,1)S(1)} %collective-permute-done.11.refs_3_, ...), custom_call_target="tpu_custom_call" | custom-call | tf_op jit(solution)/shard_map/pallas_call | solution.py:226
  46.0 0.0 collective-permute-done.12.refs_5_
  46.0 0.0 collective-permute-done.10.refs_4_
  46.0 1.1 %shard_map.43 = f32[16,2,128]{2,1,0:T(2,128)S(1)} custom-call(bf16[256,768]{1,0:T(8,128)(2,1)S(1)} %pad_maximum_fusion.refs_0_, bf16[256,768]{1,0:T(8,128)(2,1)S(1)} %pad_maximum_fusion.1.refs_1_, bf16[256,768]{1,0:T(8,128)(2,1)S(1)} %collective-permute-done.6.refs_4_.refs_2_, bf16[256,768]{1,0:T(8,128)(2,1)S(1)} %collective-permute-done.7.refs_4_.refs_3_, ...), custom_call_target="tpu_custom_call" | custom-call | tf_op jit(solution)/shard_map/pallas_call | solution.py:226
  47.1 11.2 %all_to_all.10.returned_ref = f32[16,2,128]{2,1,0:T(2,128)S(1)} all-to-all(f32[16,2,128]{2,1,0:T(2,128)S(1)} %shard_map.43), channel_id=1, replica_groups=mesh['grp'=2,'dev'=16] {'dev'}, dimensions={0} | all-to-all | bytes 32768 | tf_op jit(solution)/shard_map/all_to_all | solution.py:422
  58.3 1.2 %shard_map.44 = f32[1,512]{1,0:T(1,128)} custom-call(s32[2,512]{1,0:T(2,128)S(1)} %get-tuple-element.17.rank_ref, f32[16,2,128]{2,1,0:T(2,128)S(1)} %all_to_all.10.returned_ref), custom_call_target="tpu_custom_call" | custom-call | tf_op jit(solution)/shard_map/pallas_call | solution.py:423
  (31 shorter events, 0.4 us)
Async XLA Ops:
  0.0 1.1 %copy-start = (bf16[512,768]{1,0:T(8,128)(2,1)S(1)}, bf16[512,768]{1,0:T(8,128)(2,1)}, u32[]{:S(2)}) copy-start(bf16[512,768]{1,0:T(8,128)(2,1)} %rows_hbm.1) | copy-start | bytes 2359300
  1.1 0.7 %copy-start.1 = (s32[512]{0:T(512)S(1)}, s32[512]{0:T(512)}, u32[]{:S(2)}) copy-start(s32[512]{0:T(512)} %param.4) | copy-start | bytes 6148
  2.9 11.4 %collective-permute-start = (bf16[128,768]{1,0:T(8,128)(2,1)S(1)}, bf16[128,768]{1,0:T(8,128)(2,1)S(1)}, u32[]{:S(2)}, u32[]{:S(2)}) collective-permute-start(bf16[128,768]{1,0:T(8,128)(2,1)S(1)} %get-tuple-element.19.refs_2_), channel_id=1, source_target_pairs={{0,4},{1,5},{2,6},{3,7},{4,0},{5,1},{6,2},{7,3},{8,12},{9,13},{10,... | collective-permute-start | bytes 589832 | tf_op jit(solution)/shard_map/ppermute | solution.py:280
  5.9 14.0 %collective-permute-start.1 = (bf16[64,768]{1,0:T(8,128)(2,1)S(1)}, bf16[64,768]{1,0:T(8,128)(2,1)S(1)}, u32[]{:S(2)}, u32[]{:S(2)}) collective-permute-start(bf16[64,768]{1,0:T(8,128)(2,1)S(1)} %get-tuple-element.20.refs_3_), channel_id=1, source_target_pairs={{0,8},{1,9},{2,10},{3,11},{4,12},{5,13},{6,14},{7,15},{8,0},{9,1},... | collective-permute-start | bytes 294920 | tf_op jit(solution)/shard_map/ppermute | solution.py:280
  8.5 11.4 %collective-permute-start.2 = (bf16[64,768]{1,0:T(8,128)(2,1)S(1)}, bf16[64,768]{1,0:T(8,128)(2,1)S(1)}, u32[]{:S(2)}, u32[]{:S(2)}) collective-permute-start(bf16[64,768]{1,0:T(8,128)(2,1)S(1)} %get-tuple-element.21.refs_5_), channel_id=1, source_target_pairs={{0,12},{1,13},{2,14},{3,15},{4,8},{5,9},{6,10},{7,11},{8,4},{9,5},... | collective-permute-start | bytes 294920 | tf_op jit(solution)/shard_map/ppermute | solution.py:280
  8.5 19.4 %collective-permute-start.3 = (bf16[64,768]{1,0:T(8,128)(2,1)S(1)}, bf16[64,768]{1,0:T(8,128)(2,1)S(1)}, u32[]{:S(2)}, u32[]{:S(2)}) collective-permute-start(bf16[64,768]{1,0:T(8,128)(2,1)S(1)} %get-tuple-element.23.refs_4_), channel_id=1, source_target_pairs={{0,8},{1,9},{2,10},{3,11},{4,12},{5,13},{6,14},{7,15},{8,0},{9,1},... | collective-permute-start | bytes 294920 | tf_op jit(solution)/shard_map/ppermute | solution.py:280
  10.4 17.5 %collective-permute-start.4 = (bf16[64,768]{1,0:T(8,128)(2,1)S(1)}, bf16[64,768]{1,0:T(8,128)(2,1)S(1)}, u32[]{:S(2)}, u32[]{:S(2)}) collective-permute-start(bf16[64,768]{1,0:T(8,128)(2,1)S(1)} %get-tuple-element.24.refs_6_), channel_id=1, source_target_pairs={{0,12},{1,13},{2,14},{3,15},{4,8},{5,9},{6,10},{7,11},{8,4},{9,5},... | collective-permute-start | bytes 294920 | tf_op jit(solution)/shard_map/ppermute | solution.py:280
  12.4 0.7 %copy-start.2 = (s32[512]{0:T(512)S(1)}, s32[512]{0:T(512)}, u32[]{:S(2)}) copy-start(s32[512]{0:T(512)} %param.5) | copy-start | bytes 6148
  14.2 14.0 %all-to-all-start = ((f32[16,8,128]{2,1,0:T(8,128)}), f32[16,8,128]{2,1,0:T(8,128)S(1)}, u32[]{:S(2)}, u32[]{:S(2)}) async-start(f32[16,8,128]{2,1,0:T(8,128)} %shard_map.38), calls=%async_computation | async-start | bytes 131072 | tf_op jit(solution)/shard_map/all_to_all | solution.py:345
  20.0 9.7 %collective-permute-start.5 = (bf16[256,768]{1,0:T(8,128)(2,1)S(1)}, bf16[256,768]{1,0:T(8,128)(2,1)S(1)}, u32[]{:S(2)}, u32[]{:S(2)}) collective-permute-start(bf16[256,768]{1,0:T(8,128)(2,1)S(1)} %pad_maximum_fusion.refs_0_), channel_id=1, source_target_pairs={{0,1},{1,0},{2,3},{3,2},{4,5},{5,4},{6,7},{7,6},{8,9},{9,8},{10,11... | collective-permute-start | bytes 1179656 | tf_op jit(solution)/shard_map/ppermute | solution.py:280
  20.5 11.9 %collective-permute-start.6 = (bf16[256,768]{1,0:T(8,128)(2,1)S(1)}, bf16[256,768]{1,0:T(8,128)(2,1)S(1)}, u32[]{:S(2)}, u32[]{:S(2)}) collective-permute-start(bf16[256,768]{1,0:T(8,128)(2,1)S(1)} %pad_maximum_fusion.refs_0_), channel_id=1, source_target_pairs={{0,2},{1,3},{2,0},{3,1},{4,6},{5,7},{6,4},{7,5},{8,10},{9,11},{10,... | collective-permute-start | bytes 1179656 | tf_op jit(solution)/shard_map/ppermute | solution.py:280
  22.2 13.7 %collective-permute-start.8 = (bf16[256,768]{1,0:T(8,128)(2,1)S(1)}, bf16[256,768]{1,0:T(8,128)(2,1)}, u32[]{:S(2)}, u32[]{:S(2)}) collective-permute-start(bf16[256,768]{1,0:T(8,128)(2,1)S(1)} %pad_maximum_fusion.refs_0_), channel_id=1, source_target_pairs={{0,4},{1,5},{2,6},{3,7},{4,8},{5,9},{6,10},{7,11},{8,12},{9,13},{1... | collective-permute-start | bytes 1179656 | tf_op jit(solution)/shard_map/ppermute | solution.py:284
  29.7 2.7 %collective-permute-start.11 = (bf16[256,768]{1,0:T(8,128)(2,1)S(1)}, bf16[256,768]{1,0:T(8,128)(2,1)S(1)}, u32[]{:S(2)}, u32[]{:S(2)}) collective-permute-start(bf16[256,768]{1,0:T(8,128)(2,1)S(1)} %pad_maximum_fusion.1.refs_1_), channel_id=1, source_target_pairs={{0,1},{1,0},{2,3},{3,2},{4,5},{5,4},{6,7},{7,6},{8,9},{9,8},{10,11... | collective-permute-start | bytes 1179656 | tf_op jit(solution)/shard_map/ppermute | solution.py:280
  29.8 13.5 %collective-permute-start.9 = (bf16[256,768]{1,0:T(8,128)(2,1)S(1)}, bf16[256,768]{1,0:T(8,128)(2,1)}, u32[]{:S(2)}, u32[]{:S(2)}) collective-permute-start(bf16[256,768]{1,0:T(8,128)(2,1)S(1)} %pad_maximum_fusion.1.refs_1_), channel_id=1, source_target_pairs={{4,0},{5,1},{6,2},{7,3},{8,4},{9,5},{10,6},{11,7},{12,8},{13,9},{1... | collective-permute-start | bytes 1179656 | tf_op jit(solution)/shard_map/ppermute | solution.py:284
  31.6 12.2 %collective-permute-start.7 = (bf16[256,768]{1,0:T(8,128)(2,1)S(1)}, bf16[256,768]{1,0:T(8,128)(2,1)S(1)}, u32[]{:S(2)}, u32[]{:S(2)}) collective-permute-start(bf16[256,768]{1,0:T(8,128)(2,1)S(1)} %pad_maximum_fusion.1.refs_1_), channel_id=1, source_target_pairs={{0,2},{1,3},{2,0},{3,1},{4,6},{5,7},{6,4},{7,5},{8,10},{9,11},{10,... | collective-permute-start | bytes 1179656 | tf_op jit(solution)/shard_map/ppermute | solution.py:280
  43.3 2.7 %collective-permute-start.12 = (bf16[256,768]{1,0:T(8,128)(2,1)}, bf16[256,768]{1,0:T(8,128)(2,1)S(1)}, u32[]{:S(2)}, u32[]{:S(2)}) collective-permute-start(bf16[256,768]{1,0:T(8,128)(2,1)} %collective-permute-done.9.refs_6_), channel_id=1, source_target_pairs={{0,1},{1,0},{2,3},{3,2},{4,5},{5,4},{6,7},{7,6},{8,9},{9,8},{10,11... | collective-permute-start | bytes 1179656 | tf_op jit(solution)/shard_map/ppermute | solution.py:280
  43.3 2.7 %collective-permute-start.10 = (bf16[256,768]{1,0:T(8,128)(2,1)}, bf16[256,768]{1,0:T(8,128)(2,1)S(1)}, u32[]{:S(2)}, u32[]{:S(2)}) collective-permute-start(bf16[256,768]{1,0:T(8,128)(2,1)} %collective-permute-done.8.refs_3_.refs_5_), channel_id=1, source_target_pairs={{0,1},{1,0},{2,3},{3,2},{4,5},{5,4},{6,7},{7,6},{8,9},{9,8},{10,11... | collective-permute-start | bytes 1179656 | tf_op jit(solution)/shard_map/ppermute | solution.py:280

commit v5 on v0

--- a/solution.py
+++ b/solution.py
@@ -222,7 +222,11 @@
     return call(
         kernel,
         jax.ShapeDtypeStruct(layout or (len(SUMS), n), jnp.float32),
-        cost_estimate=pl.CostEstimate(flops=0, transcendentals=0, bytes_accessed=0),
+        cost_estimate=pl.CostEstimate(
+            flops=2 * len(jobs) * n * n * width,
+            transcendentals=len(jobs) * n * n,
+            bytes_accessed=2 * len(names) * n * width,
+        ),
     )(*operands)
 
 

time: 60 us -> 58.8 us (0.980)
  Pallas kernels: 12.7 us -> 10.3 us
  waiting for transfers between devices: 7.93 us -> 9.28 us
    pallas_call x4, Pallas kernels: 8.6 us -> 6.27 us  [masses_call(): call(kernel, jax.ShapeDtypeStruct(layout or (len(SUMS), n), jnp.float32),...]
    ppermute x11, waiting for transfers between devices: 1.33 us -> 2.68 us  [swapped(): return lax.ppermute(rows_, 'dev', [(i, i ^ bit) for i in range(peers)])]
  transfers between devices with their start and end apart: 14 -> 14, of which waited for: 5 -> 5; matrix products, arithmetic and copies ran while one was open for 2% -> 2% of each run, Pallas kernels for 14% -> 12%
where the time goes in v5:
time: 58.8 us; the launch traced here: 58.4 us
  starting transfers between devices  23.8 us (40%)
  Pallas kernels  10.3 us (18%)
  blocking collectives  10.3 us (18%)
  waiting for transfers between devices  9.28 us (16%)
  local copies, waits for them, and re-layouts  4.12 us (7%)
    ppermute x11, starting transfers between devices, swapped(): return lax.ppermute(rows_, 'dev', [(i, i ^ bit) for i in range(peers)])  12.4 us
    all_to_all x1, blocking collectives, shards(): lax.all_to_all(outgoing, 'dev', split_axis=0, concat_axis=0, tiled=True)  10.3 us
    ppermute x2, starting transfers between devices, passed(): return lax.ppermute(rows_, 'dev', pairs)  6.34 us
    pallas_call x4, Pallas kernels, masses_call(): call(kernel, jax.ShapeDtypeStruct(layout or (len(SUMS), n), jnp.float32),...  6.27 us
    ppermute x2, waiting for transfers between devices, passed(): return lax.ppermute(rows_, 'dev', pairs)  5.64 us
    all_to_all x1, starting transfers between devices, shards(): lax.all_to_all(facts, 'dev', split_axis=0, concat_axis=0, tiled=True)  5.02 us
    unnamed x9, local copies, waits for them, and re-layouts  3.18 us
    ppermute x11, waiting for transfers between devices, swapped(): return lax.ppermute(rows_, 'dev', [(i, i ^ bit) for i in range(peers)])  2.68 us
  transfers between devices with their start and end apart: 14, of which 5 were waited for; matrix products, arithmetic and copies ran while one was open for 2% of the time, Pallas kernels for 12%

profile of v5, /device:TPU:0, one launch (start us, length us, event | category | flops | bytes accessed | tf_op | source)
XLA Modules:
  0.0 58.4 jit_solution(18061608445480473213)
XLA Ops:
  0.0 0.0 copy-start
  0.0 1.1 %copy-done = bf16[512,768]{1,0:T(8,128)(2,1)S(1)} copy-done((bf16[512,768]{1,0:T(8,128)(2,1)S(1)}, bf16[512,768]{1,0:T(8,128)(2,1)}, u32[]{:S(2)}) %copy-start) | copy-done | bytes 786456
  1.1 0.0 copy-start.1
  1.1 0.7 %copy-done.1 = s32[512]{0:T(512)S(1)} copy-done((s32[512]{0:T(512)S(1)}, s32[512]{0:T(512)}, u32[]{:S(2)}) %copy-start.1) | copy-done | bytes 2072
  1.8 1.0 %shard_map.37 = (bf16[64,768]{1,0:T(8,128)(2,1)S(1)}, bf16[64,768]{1,0:T(8,128)(2,1)S(1)}, bf16[128,768]{1,0:T(8,128)(2,1)S(1)}, bf16[64,768]{1,0:T(8,128)(2,1)S...) custom-call(s32[1,512]{1,0:T(1,128)S(1)} %bitcast.27, ...), custom_call_target="tpu_custom_call" | custom-call | tf_op jit(solution)/shard_map/pallas_call | solution.py:294
  2.9 3.1 %collective-permute-start = (bf16[128,768]{1,0:T(8,128)(2,1)S(1)}, bf16[128,768]{1,0:T(8,128)(2,1)S(1)}, u32[]{:S(2)}, u32[]{:S(2)}) collective-permute-start(bf16[128,768]{1,0:T(8,128)(2,1)S(1)} %get-tuple-element.19.refs_2_), channel_id=1, source_target_pairs={{0,4},{1,5},{2,6},{3,7},{4,0},{5,1},{6,2},{7,3},{8,12},{9,13},{10,... | collective-permute-start | bytes 589832 | tf_op jit(solution)/shard_map/ppermute | solution.py:280
  5.9 2.6 %collective-permute-start.3 = (bf16[64,768]{1,0:T(8,128)(2,1)S(1)}, bf16[64,768]{1,0:T(8,128)(2,1)S(1)}, u32[]{:S(2)}, u32[]{:S(2)}) collective-permute-start(bf16[64,768]{1,0:T(8,128)(2,1)S(1)} %get-tuple-element.23.refs_3_), channel_id=1, source_target_pairs={{0,8},{1,9},{2,10},{3,11},{4,12},{5,13},{6,14},{7,15},{8,0},{9,1},... | collective-permute-start | bytes 294920 | tf_op jit(solution)/shard_map/ppermute | solution.py:280
  8.5 0.0 collective-permute-start.4
  8.5 1.9 %collective-permute-start.1 = (bf16[64,768]{1,0:T(8,128)(2,1)S(1)}, bf16[64,768]{1,0:T(8,128)(2,1)S(1)}, u32[]{:S(2)}, u32[]{:S(2)}) collective-permute-start(bf16[64,768]{1,0:T(8,128)(2,1)S(1)} %get-tuple-element.20.refs_4_), channel_id=1, source_target_pairs={{0,8},{1,9},{2,10},{3,11},{4,12},{5,13},{6,14},{7,15},{8,0},{9,1},... | collective-permute-start | bytes 294920 | tf_op jit(solution)/shard_map/ppermute | solution.py:280
  10.4 1.9 %collective-permute-start.2 = (bf16[64,768]{1,0:T(8,128)(2,1)S(1)}, bf16[64,768]{1,0:T(8,128)(2,1)S(1)}, u32[]{:S(2)}, u32[]{:S(2)}) collective-permute-start(bf16[64,768]{1,0:T(8,128)(2,1)S(1)} %get-tuple-element.21.refs_6_), channel_id=1, source_target_pairs={{0,12},{1,13},{2,14},{3,15},{4,8},{5,9},{6,10},{7,11},{8,4},{9,5},... | collective-permute-start | bytes 294920 | tf_op jit(solution)/shard_map/ppermute | solution.py:280
  12.4 0.0 copy-start.2
  12.4 0.7 %copy-done.2 = s32[512]{0:T(512)S(1)} copy-done((s32[512]{0:T(512)S(1)}, s32[512]{0:T(512)}, u32[]{:S(2)}) %copy-start.2) | copy-done | bytes 2072
  13.0 0.0 copy-start.3
  13.0 0.7 %copy-done.3 = s32[512]{0:T(512)S(1)} copy-done((s32[512]{0:T(512)S(1)}, s32[512]{0:T(512)}, u32[]{:S(2)}) %copy-start.3) | copy-done | bytes 2072
  13.7 1.2 %shard_map.38 = f32[16,8,128]{2,1,0:T(8,128)} custom-call(s32[1,512]{1,0:T(1,128)S(1)} %bitcast.28, s32[1,512]{1,0:T(1,128)S(1)} %bitcast.29, s32[1,512]{1,0:T(1,128)S(1)} %get-tuple-element.17.rank_ref, bf16[64,768]{1,0:T(8,128)(2,1)S(1)} %get-tuple-element.22.refs_0_, bf16[64,768]{1,0:T(8,128)(2,1)S(1)} %get-tuple-element.18.refs_1_, ...), custom_call_target="tpu_custom_call" | custom-call | tf_op jit(solution)/shard_map/pallas_call | solution.py:325
  14.9 0.0 collective-permute-done
  14.9 5.0 %all-to-all-start = ((f32[16,8,128]{2,1,0:T(8,128)}), f32[16,8,128]{2,1,0:T(8,128)S(1)}, u32[]{:S(2)}, u32[]{:S(2)}) async-start(f32[16,8,128]{2,1,0:T(8,128)} %shard_map.38), calls=%async_computation | async-start | bytes 131072 | tf_op jit(solution)/shard_map/all_to_all | solution.py:342
  20.0 0.0 collective-permute-done.3
  20.0 0.0 collective-permute-done.4
  20.0 0.5 collective-permute-start.5
  20.5 1.7 %collective-permute-start.8 = (bf16[256,768]{1,0:T(8,128)(2,1)S(1)}, bf16[256,768]{1,0:T(8,128)(2,1)S(1)}, u32[]{:S(2)}, u32[]{:S(2)}) collective-permute-start(bf16[256,768]{1,0:T(8,128)(2,1)S(1)} %pad_maximum_fusion.1.refs_0_), channel_id=1, source_target_pairs={{0,2},{1,3},{2,0},{3,1},{4,6},{5,7},{6,4},{7,5},{8,10},{9,11},{10,... | collective-permute-start | bytes 1179656 | tf_op jit(solution)/shard_map/ppermute | solution.py:280
  22.2 5.1 %collective-permute-start.9 = (bf16[256,768]{1,0:T(8,128)(2,1)S(1)}, bf16[256,768]{1,0:T(8,128)(2,1)S(1)}, u32[]{:S(2)}, u32[]{:S(2)}) collective-permute-start(bf16[256,768]{1,0:T(8,128)(2,1)S(1)} %pad_maximum_fusion.1.refs_0_), channel_id=1, source_target_pairs={{0,4},{1,5},{2,6},{3,7},{4,8},{5,9},{6,10},{7,11},{8,12},{9,13},{1... | collective-permute-start | bytes 1179656 | tf_op jit(solution)/shard_map/ppermute | solution.py:284
  27.2 0.0 collective-permute-done.1
  27.2 0.0 collective-permute-done.2
  27.3 1.0 %all-to-all-done = f32[16,8,128]{2,1,0:T(8,128)S(1)} async-done(((f32[16,8,128]{2,1,0:T(8,128)}), f32[16,8,128]{2,1,0:T(8,128)S(1)}, u32[]{:S(2)}, u32[]{:S(2)}) %all-to-all-start) | async-done | bytes 65568 | tf_op jit(solution)/shard_map/all_to_all | solution.py:342
  28.3 0.1 reshape_reshape.15
  28.6 0.1 reshape.133
  28.7 0.1 rev.32
  28.9 0.1 reshape.132
  29.0 0.6 %shard_map.39 = f32[1,2560]{1,0:T(1,128)S(1)} custom-call(s32[1,2560]{1,0:T(1,128)S(1)} %fusion.2.place_ref, f32[48,128]{1,0:T(8,128)S(1)} %fusion.1.table_ref), custom_call_target="tpu_custom_call" | custom-call | tf_op jit(solution)/shard_map/pallas_call | solution.py:373
  29.7 0.0 collective-permute-done.5.refs_2_
  29.7 0.1 collective-permute-start.11
  29.8 0.4 copy.16.refs_6_.refs_8_.refs_5_
  30.3 0.7 %collective-permute-start.6 = (bf16[256,768]{1,0:T(8,128)(2,1)S(1)}, bf16[256,768]{1,0:T(8,128)(2,1)S(1)}, u32[]{:S(2)}, u32[]{:S(2)}) collective-permute-start(bf16[256,768]{1,0:T(8,128)(2,1)S(1)} %pad_maximum_fusion.refs_1_.refs_0_), channel_id=1, source_target_pairs={{0,2},{1,3},{2,0},{3,1},{4,6},{5,7},{6,4},{7,5},{8,10},{9,11},{10,... | collective-permute-start | bytes 1179656 | tf_op jit(solution)/shard_map/ppermute | solution.py:280
  31.0 1.3 %collective-permute-start.7 = (bf16[256,768]{1,0:T(8,128)(2,1)S(1)}, bf16[256,768]{1,0:T(8,128)(2,1)S(1)}, u32[]{:S(2)}, u32[]{:S(2)}) collective-permute-start(bf16[256,768]{1,0:T(8,128)(2,1)S(1)} %pad_maximum_fusion.refs_1_.refs_0_), channel_id=1, source_target_pairs={{4,0},{5,1},{6,2},{7,3},{8,4},{9,5},{10,6},{11,7},{12,8},{13,9},{1... | collective-permute-start | bytes 1179656 | tf_op jit(solution)/shard_map/ppermute | solution.py:284
  32.2 0.2 collective-permute-done.8.refs_4_.refs_2_
  32.4 3.5 %collective-permute-done.9.refs_3_.refs_5_ = bf16[256,768]{1,0:T(8,128)(2,1)S(1)} collective-permute-done((bf16[256,768]{1,0:T(8,128)(2,1)S(1)}, bf16[256,768]{1,0:T(8,128)(2,1)S(1)}, u32[]{:S(2)}, u32[]{:S(2)}) %collective-permute-start.9) | collective-permute-done | bytes 393248 | tf_op jit(solution)/shard_map/ppermute | solution.py:284
  35.9 0.0 collective-permute-start.10
  35.9 0.0 collective-permute-done.11.refs_3_
  35.9 2.4 %shard_map.40.refs_7_ = f32[8,256]{1,0:T(8,128)S(1)} custom-call(bf16[256,768]{1,0:T(8,128)(2,1)S(1)} %pad_maximum_fusion.1.refs_0_, bf16[256,768]{1,0:T(8,128)(2,1)S(1)} %pad_maximum_fusion.refs_1_.refs_0_, bf16[256,768]{1,0:T(8,128)(2,1)S(1)} %collective-permute-done.5.refs_2_, bf16[256,768]{1,0:T(8,128)(2,1)} %collective-permute-done.11.refs_3_, ...), custom_call_target="tpu_custom_call" | custom-call | flops 1107296256 | bytes 1966080 | tf_op jit(solution)/shard_map/pallas_call | solution.py:222
  38.3 0.0 collective-permute-done.10.refs_4_.refs_6_
  38.4 1.0 %shard_map.41.refs_9_ = f32[8,256]{1,0:T(8,128)S(1)} custom-call(bf16[256,768]{1,0:T(8,128)(2,1)S(1)} %pad_maximum_fusion.1.refs_0_, bf16[256,768]{1,0:T(8,128)(2,1)S(1)} %pad_maximum_fusion.refs_1_.refs_0_, bf16[256,768]{1,0:T(8,128)(2,1)S(1)} %collective-permute-done.8.refs_4_.refs_2_, bf16[256,768]{1,0:T(8,128)(2,1)S(1)} %collective-permute-done.9.refs_3_.refs_5_, ...), custom_call_target="tpu_custom_call" | custom-call | flops 603979776 | bytes 1966080 | tf_op jit(solution)/shard_map/pallas_call | solution.py:222
  39.4 2.5 %collective-permute-done.6.refs_4_.refs_1_ = bf16[256,768]{1,0:T(8,128)(2,1)S(1)} collective-permute-done((bf16[256,768]{1,0:T(8,128)(2,1)S(1)}, bf16[256,768]{1,0:T(8,128)(2,1)S(1)}, u32[]{:S(2)}, u32[]{:S(2)}) %collective-permute-start.6) | collective-permute-done | bytes 393248 | tf_op jit(solution)/shard_map/ppermute | solution.py:280
  41.9 2.1 %collective-permute-done.7.refs_2_ = bf16[256,768]{1,0:T(8,128)(2,1)S(1)} collective-permute-done((bf16[256,768]{1,0:T(8,128)(2,1)S(1)}, bf16[256,768]{1,0:T(8,128)(2,1)S(1)}, u32[]{:S(2)}, u32[]{:S(2)}) %collective-permute-start.7) | collective-permute-done | bytes 393248 | tf_op jit(solution)/shard_map/ppermute | solution.py:284
  44.0 0.0 collective-permute-start.12
  44.0 2.0 %shard_map.42.refs_6_ = f32[8,256]{1,0:T(8,128)S(1)} custom-call(bf16[256,768]{1,0:T(8,128)(2,1)S(1)} %pad_maximum_fusion.1.refs_0_, bf16[256,768]{1,0:T(8,128)(2,1)S(1)} %pad_maximum_fusion.refs_1_.refs_0_, bf16[256,768]{1,0:T(8,128)(2,1)S(1)} %collective-permute-done.5.refs_2_, bf16[256,768]{1,0:T(8,128)(2,1)} %collective-permute-done.11.refs_3_, ...), custom_call_target="tpu_custom_call" | custom-call | flops 603979776 | bytes 2752512 | tf_op jit(solution)/shard_map/pallas_call | solution.py:222
  46.0 0.0 collective-permute-done.12.refs_3_
  46.0 0.9 %shard_map.43 = f32[16,2,128]{2,1,0:T(2,128)S(1)} custom-call(bf16[256,768]{1,0:T(8,128)(2,1)S(1)} %pad_maximum_fusion.refs_1_.refs_0_, bf16[256,768]{1,0:T(8,128)(2,1)S(1)} %collective-permute-done.6.refs_4_.refs_1_, bf16[256,768]{1,0:T(8,128)(2,1)S(1)} %collective-permute-done.7.refs_2_, bf16[256,768]{1,0:T(8,128)(2,1)S(1)} %collective-permute-done.12.refs_3_, ...), custom_call_target="tpu_custom_call" | custom-call | flops 402653184 | bytes 1572864 | tf_op jit(solution)/shard_map/pallas_call | solution.py:222
  46.9 10.3 %all_to_all.10.returned_ref = f32[16,2,128]{2,1,0:T(2,128)S(1)} all-to-all(f32[16,2,128]{2,1,0:T(2,128)S(1)} %shard_map.43), channel_id=1, replica_groups=mesh['grp'=2,'dev'=16] {'dev'}, dimensions={0} | all-to-all | bytes 32768 | tf_op jit(solution)/shard_map/all_to_all | solution.py:418
  57.2 1.2 %shard_map.44 = f32[1,512]{1,0:T(1,128)} custom-call(s32[1,512]{1,0:T(1,128)S(1)} %get-tuple-element.17.rank_ref, f32[16,2,128]{2,1,0:T(2,128)S(1)} %all_to_all.10.returned_ref), custom_call_target="tpu_custom_call" | custom-call | tf_op jit(solution)/shard_map/pallas_call | solution.py:419
  (31 shorter events, 0.4 us)
Async XLA Ops:
  0.0 1.1 %copy-start = (bf16[512,768]{1,0:T(8,128)(2,1)S(1)}, bf16[512,768]{1,0:T(8,128)(2,1)}, u32[]{:S(2)}) copy-start(bf16[512,768]{1,0:T(8,128)(2,1)} %rows_hbm.1) | copy-start | bytes 2359300
  1.1 0.7 %copy-start.1 = (s32[512]{0:T(512)S(1)}, s32[512]{0:T(512)}, u32[]{:S(2)}) copy-start(s32[512]{0:T(512)} %param.4) | copy-start | bytes 6148
  2.9 12.0 %collective-permute-start = (bf16[128,768]{1,0:T(8,128)(2,1)S(1)}, bf16[128,768]{1,0:T(8,128)(2,1)S(1)}, u32[]{:S(2)}, u32[]{:S(2)}) collective-permute-start(bf16[128,768]{1,0:T(8,128)(2,1)S(1)} %get-tuple-element.19.refs_2_), channel_id=1, source_target_pairs={{0,4},{1,5},{2,6},{3,7},{4,0},{5,1},{6,2},{7,3},{8,12},{9,13},{10,... | collective-permute-start | bytes 589832 | tf_op jit(solution)/shard_map/ppermute | solution.py:280
  5.9 14.0 %collective-permute-start.3 = (bf16[64,768]{1,0:T(8,128)(2,1)S(1)}, bf16[64,768]{1,0:T(8,128)(2,1)S(1)}, u32[]{:S(2)}, u32[]{:S(2)}) collective-permute-start(bf16[64,768]{1,0:T(8,128)(2,1)S(1)} %get-tuple-element.23.refs_3_), channel_id=1, source_target_pairs={{0,8},{1,9},{2,10},{3,11},{4,12},{5,13},{6,14},{7,15},{8,0},{9,1},... | collective-permute-start | bytes 294920 | tf_op jit(solution)/shard_map/ppermute | solution.py:280
  8.5 11.4 %collective-permute-start.4 = (bf16[64,768]{1,0:T(8,128)(2,1)S(1)}, bf16[64,768]{1,0:T(8,128)(2,1)S(1)}, u32[]{:S(2)}, u32[]{:S(2)}) collective-permute-start(bf16[64,768]{1,0:T(8,128)(2,1)S(1)} %get-tuple-element.24.refs_5_), channel_id=1, source_target_pairs={{0,12},{1,13},{2,14},{3,15},{4,8},{5,9},{6,10},{7,11},{8,4},{9,5},... | collective-permute-start | bytes 294920 | tf_op jit(solution)/shard_map/ppermute | solution.py:280
  8.5 18.7 %collective-permute-start.1 = (bf16[64,768]{1,0:T(8,128)(2,1)S(1)}, bf16[64,768]{1,0:T(8,128)(2,1)S(1)}, u32[]{:S(2)}, u32[]{:S(2)}) collective-permute-start(bf16[64,768]{1,0:T(8,128)(2,1)S(1)} %get-tuple-element.20.refs_4_), channel_id=1, source_target_pairs={{0,8},{1,9},{2,10},{3,11},{4,12},{5,13},{6,14},{7,15},{8,0},{9,1},... | collective-permute-start | bytes 294920 | tf_op jit(solution)/shard_map/ppermute | solution.py:280
  10.4 16.8 %collective-permute-start.2 = (bf16[64,768]{1,0:T(8,128)(2,1)S(1)}, bf16[64,768]{1,0:T(8,128)(2,1)S(1)}, u32[]{:S(2)}, u32[]{:S(2)}) collective-permute-start(bf16[64,768]{1,0:T(8,128)(2,1)S(1)} %get-tuple-element.21.refs_6_), channel_id=1, source_target_pairs={{0,12},{1,13},{2,14},{3,15},{4,8},{5,9},{6,10},{7,11},{8,4},{9,5},... | collective-permute-start | bytes 294920 | tf_op jit(solution)/shard_map/ppermute | solution.py:280
  12.4 0.7 %copy-start.2 = (s32[512]{0:T(512)S(1)}, s32[512]{0:T(512)}, u32[]{:S(2)}) copy-start(s32[512]{0:T(512)} %param.4) | copy-start | bytes 6148
  13.0 0.7 %copy-start.3 = (s32[512]{0:T(512)S(1)}, s32[512]{0:T(512)}, u32[]{:S(2)}) copy-start(s32[512]{0:T(512)} %param.5) | copy-start | bytes 6148
  14.9 13.3 %all-to-all-start = ((f32[16,8,128]{2,1,0:T(8,128)}), f32[16,8,128]{2,1,0:T(8,128)S(1)}, u32[]{:S(2)}, u32[]{:S(2)}) async-start(f32[16,8,128]{2,1,0:T(8,128)} %shard_map.38), calls=%async_computation | async-start | bytes 131072 | tf_op jit(solution)/shard_map/all_to_all | solution.py:342
  20.0 9.7 %collective-permute-start.5 = (bf16[256,768]{1,0:T(8,128)(2,1)S(1)}, bf16[256,768]{1,0:T(8,128)(2,1)S(1)}, u32[]{:S(2)}, u32[]{:S(2)}) collective-permute-start(bf16[256,768]{1,0:T(8,128)(2,1)S(1)} %pad_maximum_fusion.1.refs_0_), channel_id=1, source_target_pairs={{0,1},{1,0},{2,3},{3,2},{4,5},{5,4},{6,7},{7,6},{8,9},{9,8},{10,11... | collective-permute-start | bytes 1179656 | tf_op jit(solution)/shard_map/ppermute | solution.py:280
  20.5 11.9 %collective-permute-start.8 = (bf16[256,768]{1,0:T(8,128)(2,1)S(1)}, bf16[256,768]{1,0:T(8,128)(2,1)S(1)}, u32[]{:S(2)}, u32[]{:S(2)}) collective-permute-start(bf16[256,768]{1,0:T(8,128)(2,1)S(1)} %pad_maximum_fusion.1.refs_0_), channel_id=1, source_target_pairs={{0,2},{1,3},{2,0},{3,1},{4,6},{5,7},{6,4},{7,5},{8,10},{9,11},{10,... | collective-permute-start | bytes 1179656 | tf_op jit(solution)/shard_map/ppermute | solution.py:280
  22.2 13.7 %collective-permute-start.9 = (bf16[256,768]{1,0:T(8,128)(2,1)S(1)}, bf16[256,768]{1,0:T(8,128)(2,1)S(1)}, u32[]{:S(2)}, u32[]{:S(2)}) collective-permute-start(bf16[256,768]{1,0:T(8,128)(2,1)S(1)} %pad_maximum_fusion.1.refs_0_), channel_id=1, source_target_pairs={{0,4},{1,5},{2,6},{3,7},{4,8},{5,9},{6,10},{7,11},{8,12},{9,13},{1... | collective-permute-start | bytes 1179656 | tf_op jit(solution)/shard_map/ppermute | solution.py:284
  29.7 6.2 %collective-permute-start.11 = (bf16[256,768]{1,0:T(8,128)(2,1)S(1)}, bf16[256,768]{1,0:T(8,128)(2,1)}, u32[]{:S(2)}, u32[]{:S(2)}) collective-permute-start(bf16[256,768]{1,0:T(8,128)(2,1)S(1)} %pad_maximum_fusion.refs_1_.refs_0_), channel_id=1, source_target_pairs={{0,1},{1,0},{2,3},{3,2},{4,5},{5,4},{6,7},{7,6},{8,9},{9,8},{10,11... | collective-permute-start | bytes 1179656 | tf_op jit(solution)/shard_map/ppermute | solution.py:280
  30.3 11.6 %collective-permute-start.6 = (bf16[256,768]{1,0:T(8,128)(2,1)S(1)}, bf16[256,768]{1,0:T(8,128)(2,1)S(1)}, u32[]{:S(2)}, u32[]{:S(2)}) collective-permute-start(bf16[256,768]{1,0:T(8,128)(2,1)S(1)} %pad_maximum_fusion.refs_1_.refs_0_), channel_id=1, source_target_pairs={{0,2},{1,3},{2,0},{3,1},{4,6},{5,7},{6,4},{7,5},{8,10},{9,11},{10,... | collective-permute-start | bytes 1179656 | tf_op jit(solution)/shard_map/ppermute | solution.py:280
  31.0 13.1 %collective-permute-start.7 = (bf16[256,768]{1,0:T(8,128)(2,1)S(1)}, bf16[256,768]{1,0:T(8,128)(2,1)S(1)}, u32[]{:S(2)}, u32[]{:S(2)}) collective-permute-start(bf16[256,768]{1,0:T(8,128)(2,1)S(1)} %pad_maximum_fusion.refs_1_.refs_0_), channel_id=1, source_target_pairs={{4,0},{5,1},{6,2},{7,3},{8,4},{9,5},{10,6},{11,7},{12,8},{13,9},{1... | collective-permute-start | bytes 1179656 | tf_op jit(solution)/shard_map/ppermute | solution.py:284
  35.9 2.5 %collective-permute-start.10 = (bf16[256,768]{1,0:T(8,128)(2,1)S(1)}, bf16[256,768]{1,0:T(8,128)(2,1)S(1)}, u32[]{:S(2)}, u32[]{:S(2)}) collective-permute-start(bf16[256,768]{1,0:T(8,128)(2,1)S(1)} %collective-permute-done.9.refs_3_.refs_5_), channel_id=1, source_target_pairs={{0,1},{1,0},{2,3},{3,2},{4,5},{5,4},{6,7},{7,6},{8,9},{9,8},{10,11... | collective-permute-start | bytes 1179656 | tf_op jit(solution)/shard_map/ppermute | solution.py:280
  44.0 2.0 %collective-permute-start.12 = (bf16[256,768]{1,0:T(8,128)(2,1)S(1)}, bf16[256,768]{1,0:T(8,128)(2,1)S(1)}, u32[]{:S(2)}, u32[]{:S(2)}) collective-permute-start(bf16[256,768]{1,0:T(8,128)(2,1)S(1)} %collective-permute-done.7.refs_2_), channel_id=1, source_target_pairs={{0,1},{1,0},{2,3},{3,2},{4,5},{5,4},{6,7},{7,6},{8,9},{9,8},{10,11... | collective-permute-start | bytes 1179656 | tf_op jit(solution)/shard_map/ppermute | solution.py:280
